TPU v7x, 256 devices: a whole 4x4x8 slice. The times are simulated.
256 devices in a mesh: grp: 8 (over y, x_hi), dev: 32 (over z, x_lo, core).
Axes of the slice: x: 4 (x_hi: 2, x_lo: 2; x = x_hi * 2 + x_lo), y: 4, z: 8, core: 2. Of those that a mesh axis runs over, the one named last changes fastest.
Arguments:
- train_grads: bfloat16 [4096, 8192], P(('grp', 'dev')), may hold values from -6 to 6
- query_grads: bfloat16 [8192, 128], P('dev'), may hold values from -6 to 6
Outputs:
- scores: float32 [4096, 128], P(('grp', 'dev'))
All inputs are finite; a program needn't handle non-finite values.
Results may differ from a plain program's by a relative error of at most 0.0037.
Values may be sent and summed in bfloat16 or wider, within the bound.
A program may use at most 64 MiB of HBM per device.

v0:
```python
import math

import jax
import jax.numpy as jnp
from jax import lax
from jax.sharding import PartitionSpec as P

ITERS = 2


DAMP = 1.0


def step_size(width, total_rows):
    bound = (1.0 + math.sqrt(width / total_rows)) ** 2
    return 1.0 / (1.0 + 1.5 * bound)


def body(train_grads, query_grads):
    group_size = lax.axis_size("dev")
    width = train_grads.shape[1]
    tile_rows = width // group_size
    owner_index = lax.axis_index("dev")
    total_rows = train_grads.shape[0] * group_size * lax.axis_size("grp")
    omega = step_size(width, total_rows)
    shard_rows = lax.all_gather(train_grads, "dev", axis=0, tiled=True)
    columns = lax.dynamic_slice_in_dim(shard_rows, owner_index * tile_rows, tile_rows, 1)
    partial_tile = lax.dot_general(
        columns, shard_rows, (((0,), (0,)), ((), ())), preferred_element_type=jnp.float32
    )
    fisher_rows = lax.psum(partial_tile, "grp") / total_rows
    query_rows = query_grads.astype(jnp.float32)
    whitened_rows = omega * query_rows
    for sweep in range(ITERS):
        applied = jnp.dot(
            fisher_rows,
            lax.all_gather(whitened_rows, "dev", axis=0, tiled=True),
            precision=lax.Precision.HIGHEST,
        )
        whitened_rows = whitened_rows + omega * (query_rows - applied - DAMP * whitened_rows)
    collect_whitened_rows = whitened_rows.astype(jnp.bfloat16)
    whitened_half = lax.all_gather(collect_whitened_rows, "dev", axis=0, tiled=True)
    return jnp.dot(train_grads, whitened_half, preferred_element_type=jnp.float32)


def solution(mesh):
    in_specs = (P(("grp", "dev"), None), P("dev", None))
    out_specs = P(("grp", "dev"), None)
    return jax.shard_map(body, mesh=mesh, in_specs=in_specs, out_specs=out_specs, check_vma=False)
```

profile of v0, /device:TPU:1, one launch (start us, length us, event | category | flops | bytes accessed | tf_op | source)
XLA Modules:
  0.0 665.1 jit_solution(13279332874879749343)
XLA Ops:
  6.5 0.0 all-gather.5.cloned.1.call-start
  6.5 0.7 all-gather.5.cloned.1.call-update
  7.3 0.0 all-gather.7.cloned.1.call-start
  7.3 1.5 convert_multiply_fusion
  8.8 0.0 all-gather.7.cloned.1.call-update
  8.8 0.0 all-reduce.2.cloned.1.call-start
  8.9 76.9 %all-gather.5.cloned.1.call-done = bf16[512,8192]{1,0:T(8,128)(2,1)} async-done(((bf16[16,8192]{1,0:T(8,128)(2,1)}), bf16[512,8192]{1,0:T(8,128)(2,1)}) %all-gather.5.cloned.1.call-update) | async-done | bytes 8388624 | tf_op jit(solution)/shard_map/all_gather | solution.py:26
  85.8 9.1 %fusion.33 = f32[256,8192]{1,0:T(8,128)} fusion(bf16[512,8192]{1,0:T(8,128)(2,1)} %all-gather.5.cloned.1.call-done, s32[]{:T(128)S(6)} %select_n.3), kind=kOutput, calls=%fused_computation.16 | convolution fusion | flops 2147483648 | bytes 17039364 | tf_op jit(solution)/shard_map/dot_general | solution.py:28
  94.9 0.0 copy-start.1
  94.9 0.0 all-reduce.2.cloned.1.call-update
  94.9 0.0 all-gather.9.cloned.1.call-start
  94.9 59.4 %all-gather.7.cloned.1.call-done = f32[8192,128]{1,0:T(8,128)} async-done(((f32[256,128]{1,0:T(8,128)}), f32[8192,128]{1,0:T(8,128)}) %all-gather.7.cloned.1.call-update) | async-done | bytes 4194320 | tf_op jit(solution)/shard_map/all_gather | solution.py:37
  154.3 348.6 %all-reduce.2.cloned.1.call-done = f32[256,8192]{1,0:T(8,128)} async-done(((f32[256,8192]{1,0:T(8,128)}), f32[256,8192]{1,0:T(8,128)}) %all-reduce.2.cloned.1.call-update) | async-done | bytes 8388624 | tf_op jit(solution)/shard_map/psum | solution.py:31
  502.9 0.0 copy-done.1
  503.0 10.5 %fusion.27 = f32[256,128]{1,0:T(8,128)} fusion(f32[8192,128]{1,0:T(8,128)} %all-gather.7.cloned.1.call-done, f32[256,8192]{1,0:T(8,128)} %all-reduce.2.cloned.1.call-done, bf16[256,128]{1,0:T(8,128)(2,1)S(1)} %copy-done.1), kind=kOutput, calls=%fused_computation.13 | convolution fusion | flops 3223519232 | bytes 12779520 | tf_op jit(solution)/shard_map/dot_general | solution.py:35
  513.5 0.0 copy-start
  513.5 0.0 all-gather.9.cloned.1.call-update
  513.5 0.0 all-gather.11.cloned.1.call-start
  513.5 67.4 %all-gather.9.cloned.1.call-done = f32[8192,128]{1,0:T(8,128)} async-done(((f32[256,128]{1,0:T(8,128)}), f32[8192,128]{1,0:T(8,128)}) %all-gather.9.cloned.1.call-update) | async-done | bytes 4194320 | tf_op jit(solution)/shard_map/all_gather | solution.py:37
  581.0 10.5 %fusion.30 = bf16[256,128]{1,0:T(8,128)(2,1)} fusion(f32[256,128]{1,0:T(8,128)} %fusion.27, f32[8192,128]{1,0:T(8,128)} %all-gather.9.cloned.1.call-done, f32[256,8192]{1,0:T(8,128)} %all-reduce.2.cloned.1.call-done, bf16[256,128]{1,0:T(8,128)(2,1)S(1)} %copy-done.1), kind=kOutput, calls=%fused_computation.14 | convolution fusion | flops 3223519232 | bytes 12845056 | tf_op jit(solution)/shard_map/dot_general | solution.py:35
  591.4 0.0 all-gather.11.cloned.1.call-update
  591.5 64.5 %all-gather.11.cloned.1.call-done = bf16[8192,128]{1,0:T(8,128)(2,1)} async-done(((bf16[256,128]{1,0:T(8,128)(2,1)}), bf16[8192,128]{1,0:T(8,128)(2,1)}) %all-gather.11.cloned.1.call-update) | async-done | bytes 2097168 | tf_op jit(solution)/shard_map/all_gather | solution.py:42
  655.9 0.0 copy-done
  655.9 2.6 convolution_bitcast_fusion
Async XLA Ops:
  6.5 79.2 %all-gather.5.cloned.1.call-start = ((), (), s32[]{:S(2)}) async-start(), calls=%async_computation | async-start | bytes 8650752 | tf_op jit(solution)/shard_map/all_gather | solution.py:26
  7.3 147.1 %all-gather.7.cloned.1.call-start = ((), (), s32[]{:S(2)}) async-start(), calls=%async_computation.2 | async-start | bytes 4325376 | tf_op jit(solution)/shard_map/all_gather | solution.py:37
  8.8 494.1 %all-reduce.2.cloned.1.call-start = ((), (), s32[]{:S(2)}) async-start(), calls=%async_computation.1 | async-start | bytes 16777216 | tf_op jit(solution)/shard_map/psum | solution.py:31
  94.9 408.1 %copy-start.1 = (bf16[256,128]{1,0:T(8,128)(2,1)S(1)}, bf16[256,128]{1,0:T(8,128)(2,1)}, u32[]{:S(2)}) copy-start(bf16[256,128]{1,0:T(8,128)(2,1)} %param.3) | copy-start | bytes 196612
  94.9 486.1 %all-gather.9.cloned.1.call-start = ((), (), s32[]{:S(2)}) async-start(), calls=%async_computation.3 | async-start | bytes 4325376 | tf_op jit(solution)/shard_map/all_gather | solution.py:37
  513.5 142.5 %copy-start = (bf16[16,8192]{1,0:T(8,128)(2,1)S(1)}, bf16[16,8192]{1,0:T(8,128)(2,1)}, u32[]{:S(2)}) copy-start(bf16[16,8192]{1,0:T(8,128)(2,1)} %param.2) | copy-start | bytes 786436
  513.5 142.5 %all-gather.11.cloned.1.call-start = ((), (), s32[]{:S(2)}) async-start(), calls=%async_computation.4 | async-start | bytes 2162688 | tf_op jit(solution)/shard_map/all_gather | solution.py:42
Sparse Core Ops, SparseCore 0:
  9.2 76.4 all-gather.4
  87.6 66.6 all-gather.6
  157.0 345.9 all-reduce.1
  513.6 67.3 all-gather.8
  591.6 64.3 all-gather.10
where the time goes:
time: 665 us
  waiting for transfers between devices  618 us (93%)
  matrix products  32.7 us (5%)
  between operations  13.1 us (2%)
    psum x1, waiting for transfers between devices, body(): fisher_rows = lax.psum(partial_tile, 'grp') / total_rows  349 us
    all_gather x2, waiting for transfers between devices, body(): lax.all_gather(whitened_rows, 'dev', axis=0, tiled=True)  127 us
    all_gather x1, waiting for transfers between devices, body(): shard_rows = lax.all_gather(train_grads, 'dev', axis=0, tiled=True)  76.9 us
    all_gather x1, waiting for transfers between devices, body(): lax.all_gather(collect_whitened_rows, 'dev', axis=0, tiled=True)  64.5 us
    dot_general x2, matrix products, body(): jnp.dot(fisher_rows, lax.all_gather(whitened_rows, 'dev', axis=0, tiled=T...  21 us
  transfers between devices with their start and end apart: 5, of which 5 were waited for; matrix products, arithmetic and copies ran while one was open for 2% of the time, Pallas kernels for 0%

commit v1 on v0

v1 whole, which is shorter than its diff:
```python
import functools
import math

import jax
import jax.numpy as jnp
from jax import lax
from jax.experimental import pallas as pl
from jax.experimental.pallas import tpu as pltpu
from jax.sharding import PartitionSpec as P

ITERS = 2
DAMP = 1.0
NX = 4
MESH = pl.DeviceIdType.MESH
F32 = jnp.float32
BF16 = jnp.bfloat16


def step_size(width, total_rows):
    bound = (1.0 + math.sqrt(width / total_rows)) ** 2
    return 1.0 / (1.0 + 1.5 * bound)


def ring(d, n):
    return min(d, n - d)


def variants(packed):
    low = lax.broadcasted_iota(jnp.int32, packed.shape, 1) < 64
    wide = packed.astype(F32)
    turned = pltpu.roll(wide, 64, 1)
    zero = jnp.zeros_like(wide)
    parts = (
        jnp.where(low, wide, zero),
        jnp.where(low, turned, zero),
        jnp.where(low, zero, turned),
        jnp.where(low, zero, wide),
    )
    return [part.astype(BF16) for part in parts]


def dot(a, b):
    return jnp.dot(a, b, preferred_element_type=F32)


def kernel(
    n_grp, n_z, omega, total_rows,
    g_ref, q_ref, o_ref,
    gbuf, gt, qbuf, qpack, send_s, recv_s, sbuf, send_t, recv_t, wbuf, wlast, send_o, recv_o,
    local_sem, send_sem, g_sem, core_sem, q_sem, rs_sem, ag_sem, rt_sem, aw_sem, o_sem,
):
    rows = g_ref.shape[0]
    block = q_ref.shape[0]
    places = 2 * n_grp
    ny = places // NX
    piece = block // n_z
    grp = lax.axis_index("grp")
    dev = lax.axis_index("dev")
    z, x_lo, core = dev // 4, lax.rem(dev // 2, 2), lax.rem(dev, 2)
    place = grp * 2 + x_lo
    y, x = place // NX, lax.rem(place, NX)

    offsets = [(dy, dx) for dy in range(ny) for dx in range(NX) if (dy, dx) != (0, 0)]
    offsets.sort(key=lambda o: -(ring(o[0], ny) + ring(o[1], NX)))
    hops = sorted(range(1, n_z), key=lambda d: -ring(d, n_z))

    def place_at(offset):
        return lax.rem(y + offset[0], ny) * NX + lax.rem(x + offset[1], NX)

    def in_plane(there, c=core):
        return (there // 2, z * 4 + lax.rem(there, 2) * 2 + c)

    def z_at(d):
        return lax.rem(z + d, n_z)

    def along_z(there, c=core):
        return (grp, there * 4 + x_lo * 2 + c)

    sibling = (grp, dev + 1 - 2 * core)

    def turned(c):
        return (z, grp * 4 + x_lo * 2 + c)

    def push(src, dst, sem, to):
        copy = pltpu.make_async_remote_copy(
            src_ref=src, dst_ref=dst, send_sem=send_sem.at[0], recv_sem=sem, device_id=to, device_id_type=MESH
        )
        copy.start()

    def arrived(like, sem):
        pltpu.make_async_copy(like, like, sem).wait()

    def row_block(p, n):
        return pl.ds(pl.multiple_of(p * n, n), n)

    barrier = pltpu.get_barrier_semaphore()
    for d in hops:
        for c in (0, 1):
            pl.semaphore_signal(barrier, inc=1, device_id=along_z(z_at(d), c), device_id_type=MESH)
    for o in offsets:
        pl.semaphore_signal(barrier, inc=1, device_id=in_plane(place_at(o)), device_id_type=MESH)
    pl.semaphore_signal(barrier, inc=1, device_id=sibling, device_id_type=MESH)

    @pl.when(z != grp)
    def _():
        for c in (0, 1):
            pl.semaphore_signal(barrier, inc=1, device_id=turned(c), device_id_type=MESH)

    others = 2 * len(hops) + len(offsets) + 1
    pl.semaphore_wait(barrier, jnp.where(z != grp, others + 2, others))

    @pl.when(z != grp)
    def _():
        for c in (0, 1):
            push(q_ref, qbuf.at[core], q_sem.at[core], turned(c))

    @pl.when(z == grp)
    def _():
        push(q_ref, qbuf.at[core], q_sem.at[core], sibling)
        pltpu.make_async_copy(q_ref, qbuf.at[core], q_sem.at[core]).start()

    width = 2 * block

    def columns(p):
        return g_ref.at[:, pl.ds(pl.multiple_of(p * width, width), width)]

    mine = gbuf.at[core, row_block(place, rows)]
    own = pltpu.make_async_copy(columns(place), mine, local_sem.at[0])
    own.start()
    for o in offsets:
        there = place_at(o)
        push(columns(there), mine, g_sem.at[0], in_plane(there))
    own.wait()
    arrived(gbuf.at[0, pl.ds(0, (places - 1) * rows)], g_sem.at[0])
    push(gbuf.at[core], gbuf.at[core], core_sem.at[0], sibling)

    arrived(qbuf.at[0], q_sem.at[0])
    arrived(qbuf.at[1], q_sem.at[1])
    top, bottom = qbuf[0].astype(F32), qbuf[1].astype(F32)
    low = lax.broadcasted_iota(jnp.int32, top.shape, 1) < 64
    first = core == 0
    packed_q = jnp.where(
        low,
        jnp.where(first, top, pltpu.roll(top, 64, 1)),
        jnp.where(first, pltpu.roll(bottom, 64, 1), bottom),
    )
    qpack[...] = packed_q.astype(BF16)
    arrived(gbuf.at[0], core_sem.at[0])

    def project(packed):
        a, b, c, d = variants(packed)
        return dot(gbuf[0], jnp.concatenate([a, b], 0)) + dot(gbuf[1], jnp.concatenate([c, d], 0))

    def back(packed):
        a, b, c, d = variants(packed)
        return dot(gt[0], jnp.concatenate([a, b], 0)) + dot(gt[1], jnp.concatenate([c, d], 0))

    my_rows = row_block(place, rows)
    my_piece = row_block(z, piece)
    query = None
    whitened = None
    for sweep in range(ITERS):
        send_s[sweep] = project(qpack[...] if sweep == 0 else wbuf[...]).astype(BF16)
        for i, o in enumerate(offsets):
            there = place_at(o)
            push(send_s.at[sweep, row_block(there, rows)], recv_s.at[sweep, i], rs_sem.at[sweep], in_plane(there))
        if sweep == 0:
            top_rows = places * rows
            for half in (0, 1):
                for part in (0, 1):
                    gt[half, :, pl.ds(part * top_rows, top_rows)] = gbuf[part, :, pl.ds(half * block, block)].T
            query = qpack[my_piece, :].astype(F32)
        arrived(recv_s.at[sweep], rs_sem.at[sweep])
        total = send_s[sweep, my_rows, :].astype(F32)
        for i in range(len(offsets)):
            total = total + recv_s[sweep, i].astype(F32)
        sbuf[sweep, my_rows, :] = total.astype(BF16)
        for o in offsets:
            there = place_at(o)
            push(sbuf.at[sweep, my_rows], sbuf.at[sweep, my_rows], ag_sem.at[sweep], in_plane(there))
        arrived(sbuf.at[sweep, pl.ds(0, (places - 1) * rows)], ag_sem.at[sweep])

        send_t[sweep] = back(sbuf[sweep]).astype(BF16)
        for i, d in enumerate(hops):
            there = z_at(d)
            push(send_t.at[sweep, row_block(there, piece)], recv_t.at[sweep, i], rt_sem.at[sweep], along_z(there))
        arrived(recv_t.at[sweep], rt_sem.at[sweep])
        total = send_t[sweep, my_piece, :].astype(F32)
        for i in range(len(hops)):
            total = total + recv_t[sweep, i].astype(F32)
        applied = total * (1.0 / total_rows)
        if sweep == 0:
            applied = omega * applied
            whitened = omega * query
        whitened = whitened + omega * (query - applied - DAMP * whitened)
        if sweep < ITERS - 1:
            wbuf[my_piece, :] = whitened.astype(BF16)
            for d in hops:
                push(wbuf.at[my_piece], wbuf.at[my_piece], aw_sem.at[0], along_z(z_at(d)))
            arrived(wbuf.at[pl.ds(0, (n_z - 1) * piece)], aw_sem.at[0])
        else:
            spot = wlast.at[core, my_piece]
            wlast[core, my_piece, :] = whitened.astype(BF16)
            for d in hops:
                for c in (0, 1):
                    push(spot, spot, aw_sem.at[1 + core], along_z(z_at(d), c))
            push(spot, spot, aw_sem.at[1 + core], sibling)
            arrived(wlast.at[0, pl.ds(0, (n_z - 1) * piece)], aw_sem.at[1 + core])
            arrived(wlast.at[0], aw_sem.at[2 - core])

    left, right = wlast[0].astype(F32), wlast[1].astype(F32)
    top = jnp.where(low, left, pltpu.roll(right, 64, 1)).astype(BF16)
    bottom = jnp.where(low, pltpu.roll(left, 64, 1), right).astype(BF16)
    send_o[...] = dot(gbuf[core], jnp.concatenate([top, bottom], 0))
    for i, o in enumerate(offsets):
        there = place_at(o)
        push(send_o.at[row_block(there, rows)], recv_o.at[i], o_sem.at[0], in_plane(there))
    arrived(recv_o, o_sem.at[0])
    total = send_o[my_rows, :]
    for i in range(len(offsets)):
        total = total + recv_o[i]
    o_ref[...] = total

    sent = send_sem.at[0]

    @pl.when(z != grp)
    def _():
        arrived(qbuf, sent)

    @pl.when(z == grp)
    def _():
        arrived(qbuf.at[0], sent)

    arrived(gbuf.at[0, pl.ds(0, (places - 1) * rows)], sent)
    arrived(gbuf.at[0], sent)
    for sweep in range(ITERS):
        arrived(recv_s.at[sweep], sent)
        arrived(sbuf.at[sweep, pl.ds(0, (places - 1) * rows)], sent)
        arrived(recv_t.at[sweep], sent)
    arrived(wbuf.at[pl.ds(0, (n_z - 1) * piece)], sent)
    arrived(wlast.at[0, pl.ds(0, (n_z - 1) * piece)], sent)
    arrived(wlast.at[0], sent)
    arrived(recv_o, sent)


def body(n_grp, n_dev, train_grads, query_grads):
    rows, width = train_grads.shape
    block, queries = query_grads.shape
    n_z = n_dev // 4
    places = 2 * n_grp
    total_rows = rows * n_grp * n_dev
    piece = block // n_z
    omega = step_size(width, total_rows)
    vmem = pl.BlockSpec(memory_space=pltpu.VMEM)
    dma = pltpu.SemaphoreType.DMA
    return pl.pallas_call(
        functools.partial(kernel, n_grp, n_z, omega, total_rows),
        name="influence",
        out_shape=jax.ShapeDtypeStruct((rows, queries), F32),
        in_specs=[vmem, vmem],
        out_specs=vmem,
        scratch_shapes=[
            pltpu.VMEM((2, places * rows, 2 * block), BF16),
            pltpu.VMEM((2, block, 2 * places * rows), BF16),
            pltpu.VMEM((2, block, queries), BF16),
            pltpu.VMEM((block, queries), BF16),
            pltpu.VMEM((ITERS, places * rows, queries), BF16),
            pltpu.VMEM((ITERS, places - 1, rows, queries), BF16),
            pltpu.VMEM((ITERS, places * rows, queries), BF16),
            pltpu.VMEM((ITERS, block, queries), BF16),
            pltpu.VMEM((ITERS, n_z - 1, piece, queries), BF16),
            pltpu.VMEM((block, queries), BF16),
            pltpu.VMEM((2, block, queries), BF16),
            pltpu.VMEM((places * rows, queries), F32),
            pltpu.VMEM((places - 1, rows, queries), F32),
            dma((1,)), dma((1,)), dma((1,)), dma((1,)), dma((2,)),
            dma((ITERS,)), dma((ITERS,)), dma((ITERS,)), dma((3,)), dma((1,)),
        ],
        compiler_params=pltpu.CompilerParams(
            collective_id=0, has_side_effects=True, vmem_limit_bytes=32 * 1024 * 1024
        ),
    )(train_grads, query_grads)


def solution(mesh):
    return jax.shard_map(
        functools.partial(body, mesh.shape["grp"], mesh.shape["dev"]),
        mesh=mesh,
        in_specs=(P(("grp", "dev"), None), P("dev", None)),
        out_specs=P(("grp", "dev"), None),
        check_vma=False,
    )
```

time: 665 us -> 73.1 us (0.11)
  waiting for transfers between devices: 618 us -> 0 us
  Pallas kernels: 0 us -> 70.5 us
  matrix products: 32.7 us -> 0 us
  between operations: 13.1 us -> 0.01 us
    psum x1 -> x0, waiting for transfers between devices: 349 us -> none  [body(): fisher_rows = lax.psum(partial_tile, 'grp') / total_rows]
    all_gather x4 -> x0, waiting for transfers between devices: 268 us -> none  [the longest x2 127 us: body(): lax.all_gather(whitened_rows, 'dev', axis=0, tiled=True)]
    pallas_call x0 -> x1, Pallas kernels: none -> 70.5 us  [body(): pl.pallas_call(functools.partial(kernel, n_grp, n_z, omega, total_rows),...]
    dot_general x4 -> x0, matrix products: 32.7 us -> none  [the longest x2 21 us: body(): jnp.dot(fisher_rows, lax.all_gather(whitened_rows, 'dev', axis=0, tiled=T...]
  transfers between devices with their start and end apart: 5 -> 0, of which waited for: 5 -> 0; matrix products, arithmetic and copies ran while one was open for 2% -> 0% of each run, Pallas kernels for 0% -> 0%
where the time goes in v1:
time: 73.1 us; the launch traced here: 72.9 us
  Pallas kernels  70.5 us (96%)
  local copies, waits for them, and re-layouts  2.39 us (3%)
    pallas_call x1, Pallas kernels, body(): pl.pallas_call(functools.partial(kernel, n_grp, n_z, omega, total_rows),...  70.5 us
    unnamed x5, local copies, waits for them, and re-layouts  2.39 us

profile of v1, /device:TPU:1, one launch (start us, length us, event | category | flops | bytes accessed | tf_op | source)
XLA Modules:
  0.0 72.9 jit_solution(2127867593475421235)
XLA Ops:
  0.0 0.0 copy-start
  0.0 0.9 %copy-done = bf16[16,8192]{1,0:T(8,128)(2,1)S(1)} copy-done((bf16[16,8192]{1,0:T(8,128)(2,1)S(1)}, bf16[16,8192]{1,0:T(8,128)(2,1)}, u32[]{:S(2)}) %copy-start) | copy-done | bytes 262168
  1.0 0.0 copy-start.1
  1.0 0.8 %copy-done.1 = bf16[256,128]{1,0:T(8,128)(2,1)S(1)} copy-done((bf16[256,128]{1,0:T(8,128)(2,1)S(1)}, bf16[256,128]{1,0:T(8,128)(2,1)}, u32[]{:S(2)}) %copy-start.1) | copy-done | bytes 65560
  1.8 70.5 %influence.1 = f32[16,128]{1,0:T(8,128)S(1)} custom-call(bf16[16,8192]{1,0:T(8,128)(2,1)S(1)} %copy-done, bf16[256,128]{1,0:T(8,128)(2,1)S(1)} %copy-done.1), custom_call_target="tpu_custom_call" | custom-call | tf_op jit(solution)/shard_map/influence/pallas_call | solution.py:256
  72.3 0.6 copy.4
Async XLA Ops:
  0.0 0.9 %copy-start = (bf16[16,8192]{1,0:T(8,128)(2,1)S(1)}, bf16[16,8192]{1,0:T(8,128)(2,1)}, u32[]{:S(2)}) copy-start(bf16[16,8192]{1,0:T(8,128)(2,1)} %g_ref.1) | copy-start | bytes 786436
  1.0 0.8 %copy-start.1 = (bf16[256,128]{1,0:T(8,128)(2,1)S(1)}, bf16[256,128]{1,0:T(8,128)(2,1)}, u32[]{:S(2)}) copy-start(bf16[256,128]{1,0:T(8,128)(2,1)} %q_ref.1) | copy-start | bytes 196612

commit v2 on v1

--- a/solution.py
+++ b/solution.py
@@ -46,7 +46,7 @@
 def kernel(
     n_grp, n_z, omega, total_rows,
     g_ref, q_ref, o_ref,
-    gbuf, gt, qbuf, qpack, send_s, recv_s, sbuf, send_t, recv_t, wbuf, wlast, send_o, recv_o,
+    gl, ql, gbuf, gt, qbuf, qpack, send_s, recv_s, sbuf, send_t, recv_t, wbuf, wlast, send_o, recv_o,
     local_sem, send_sem, g_sem, core_sem, q_sem, rs_sem, ag_sem, rt_sem, aw_sem, o_sem,
 ):
     rows = g_ref.shape[0]
@@ -81,17 +81,25 @@
     def turned(c):
         return (z, grp * 4 + x_lo * 2 + c)
 
+    leaving = []
+
     def push(src, dst, sem, to):
         copy = pltpu.make_async_remote_copy(
             src_ref=src, dst_ref=dst, send_sem=send_sem.at[0], recv_sem=sem, device_id=to, device_id_type=MESH
         )
         copy.start()
+        leaving.append(src)
 
     def arrived(like, sem):
         pltpu.make_async_copy(like, like, sem).wait()
 
     def row_block(p, n):
         return pl.ds(pl.multiple_of(p * n, n), n)
+
+    load_g = pltpu.make_async_copy(g_ref, gl, local_sem.at[1])
+    load_q = pltpu.make_async_copy(q_ref, ql, local_sem.at[2])
+    load_g.start()
+    load_q.start()
 
     barrier = pltpu.get_barrier_semaphore()
     for d in hops:
@@ -109,20 +117,25 @@
     others = 2 * len(hops) + len(offsets) + 1
     pl.semaphore_wait(barrier, jnp.where(z != grp, others + 2, others))
 
+    load_q.wait()
+    load_g.wait()
+
+    push(ql, qbuf.at[core], q_sem.at[core], turned(1 - core))
+
     @pl.when(z != grp)
     def _():
-        for c in (0, 1):
-            push(q_ref, qbuf.at[core], q_sem.at[core], turned(c))
+        push(ql, qbuf.at[core], q_sem.at[core], turned(core))
 
     @pl.when(z == grp)
     def _():
-        push(q_ref, qbuf.at[core], q_sem.at[core], sibling)
-        pltpu.make_async_copy(q_ref, qbuf.at[core], q_sem.at[core]).start()
+        pltpu.make_async_copy(ql, qbuf.at[core], q_sem.at[core]).start()
+
+    leaving.pop()
 
     width = 2 * block
 
     def columns(p):
-        return g_ref.at[:, pl.ds(pl.multiple_of(p * width, width), width)]
+        return gl.at[:, pl.ds(pl.multiple_of(p * width, width), width)]
 
     mine = gbuf.at[core, row_block(place, rows)]
     own = pltpu.make_async_copy(columns(place), mine, local_sem.at[0])
@@ -221,26 +234,12 @@
         total = total + recv_o[i]
     o_ref[...] = total
 
-    sent = send_sem.at[0]
+    for src in leaving:
+        arrived(src, send_sem.at[0])
 
     @pl.when(z != grp)
     def _():
-        arrived(qbuf, sent)
-
-    @pl.when(z == grp)
-    def _():
-        arrived(qbuf.at[0], sent)
-
-    arrived(gbuf.at[0, pl.ds(0, (places - 1) * rows)], sent)
-    arrived(gbuf.at[0], sent)
-    for sweep in range(ITERS):
-        arrived(recv_s.at[sweep], sent)
-        arrived(sbuf.at[sweep, pl.ds(0, (places - 1) * rows)], sent)
-        arrived(recv_t.at[sweep], sent)
-    arrived(wbuf.at[pl.ds(0, (n_z - 1) * piece)], sent)
-    arrived(wlast.at[0, pl.ds(0, (n_z - 1) * piece)], sent)
-    arrived(wlast.at[0], sent)
-    arrived(recv_o, sent)
+        arrived(ql, send_sem.at[0])
 
 
 def body(n_grp, n_dev, train_grads, query_grads):
@@ -252,14 +251,17 @@
     piece = block // n_z
     omega = step_size(width, total_rows)
     vmem = pl.BlockSpec(memory_space=pltpu.VMEM)
+    anywhere = pl.BlockSpec(memory_space=pl.ANY)
     dma = pltpu.SemaphoreType.DMA
     return pl.pallas_call(
         functools.partial(kernel, n_grp, n_z, omega, total_rows),
         name="influence",
         out_shape=jax.ShapeDtypeStruct((rows, queries), F32),
-        in_specs=[vmem, vmem],
+        in_specs=[anywhere, anywhere],
         out_specs=vmem,
         scratch_shapes=[
+            pltpu.VMEM((rows, width), BF16),
+            pltpu.VMEM((block, queries), BF16),
             pltpu.VMEM((2, places * rows, 2 * block), BF16),
             pltpu.VMEM((2, block, 2 * places * rows), BF16),
             pltpu.VMEM((2, block, queries), BF16),
@@ -273,11 +275,11 @@
             pltpu.VMEM((2, block, queries), BF16),
             pltpu.VMEM((places * rows, queries), F32),
             pltpu.VMEM((places - 1, rows, queries), F32),
-            dma((1,)), dma((1,)), dma((1,)), dma((1,)), dma((2,)),
+            dma((3,)), dma((1,)), dma((1,)), dma((1,)), dma((2,)),
             dma((ITERS,)), dma((ITERS,)), dma((ITERS,)), dma((3,)), dma((1,)),
         ],
         compiler_params=pltpu.CompilerParams(
-            collective_id=0, has_side_effects=True, vmem_limit_bytes=32 * 1024 * 1024
+            collective_id=0, has_side_effects=True, vmem_limit_bytes=56 * 1024 * 1024
         ),
     )(train_grads, query_grads)
 

time: 73.1 us -> 72.8 us (level)
  local copies, waits for them, and re-layouts: 2.39 us -> 1.3 us
  Pallas kernels: 70.5 us -> 71.4 us
    unnamed x5 -> x1, local copies, waits for them, and re-layouts: 2.39 us -> 1.3 us
    pallas_call x1, Pallas kernels: 70.5 us -> 71.4 us  [body(): pl.pallas_call(functools.partial(kernel, n_grp, n_z, omega, total_rows),...]
where the time goes in v2:
time: 72.8 us; the launch traced here: 72.7 us
  Pallas kernels  71.4 us (98%)
  local copies, waits for them, and re-layouts  1.3 us (2%)
    pallas_call x1, Pallas kernels, body(): pl.pallas_call(functools.partial(kernel, n_grp, n_z, omega, total_rows),...  71.4 us

profile of v2, /device:TPU:1, one launch (start us, length us, event | category | flops | bytes accessed | tf_op | source)
XLA Modules:
  0.0 72.7 jit_solution(10385420487527788075)
XLA Ops:
  0.0 71.4 %influence.1 = f32[16,128]{1,0:T(8,128)} custom-call(bf16[16,8192]{1,0:T(8,128)(2,1)} %g_ref.1, bf16[256,128]{1,0:T(8,128)(2,1)} %q_ref.1), custom_call_target="tpu_custom_call" | custom-call | tf_op jit(solution)/shard_map/influence/pallas_call | solution.py:256
  71.4 1.3 %copy.4 = f32[16,128]{1,0:T(8,128)} copy(f32[16,128]{1,0:T(8,128)} %influence.1) | data formatting | bytes 16384

commit v3 on v0

v3 whole, which is shorter than its diff:
```python
import functools
import math

import jax
import jax.numpy as jnp
from jax import lax
from jax.experimental import pallas as pl
from jax.experimental.pallas import tpu as pltpu
from jax.sharding import PartitionSpec as P

ITERS = 2
DAMP = 1.0
NX = 4
CORES = 2
SLICES = NX * CORES
MESH = pl.DeviceIdType.MESH
F32 = jnp.float32
BF16 = jnp.bfloat16


def step_size(width, total_rows):
    bound = (1.0 + math.sqrt(width / total_rows)) ** 2
    return 1.0 / (1.0 + 1.5 * bound)


def ring(d, n):
    return min(d, n - d)


def farthest_first(n):
    return sorted(range(1, n), key=lambda d: (-ring(d, n), d))


def kernel(
    n_grp, n_z, omega, total_rows,
    g_ref, q_ref, o_ref,
    gl, ql, gbuf, qb, qt, send_s, recv_s, send_t, recv_t, wlast, send_o, recv_o,
    local_sem, send_sem, q_sem, gz_sem, gx_sem, gc_sem, s_sem, t_sem, w_sem, o_sem,
):
    rows = g_ref.shape[0]
    block = q_ref.shape[0]
    width = 4 * block
    ny = n_grp * 2 // NX
    grp = lax.axis_index("grp")
    dev = lax.axis_index("dev")
    z, x_lo, core = dev // 4, lax.rem(dev // 2, 2), lax.rem(dev, 2)
    y, x = grp // 2, lax.rem(grp, 2) * 2 + x_lo
    mine = x * CORES + core

    def device(x_at, y_at, z_at, c):
        return (y_at * 2 + x_at // 2, z_at * 4 + lax.rem(x_at, 2) * 2 + c)

    def z_at(d):
        return lax.rem(z + d, n_z)

    along_z = farthest_first(n_z)
    z_partners = [device(x, y, z_at(d), core) for d in along_z]
    x_partners = [[device(lax.rem(x + d, NX), y, z, c) for c in (core, 1 - core)] for d in farthest_first(NX)]
    y_partners = [device(x, lax.rem(y + d, ny), z, core) for d in farthest_first(ny)]
    sibling = device(x, y, z, 1 - core)
    leaving = []

    def push(src, dst, sem, to):
        copy = pltpu.make_async_remote_copy(
            src_ref=src, dst_ref=dst, send_sem=send_sem.at[0], recv_sem=sem, device_id=to, device_id_type=MESH
        )
        copy.start()
        leaving.append(src)

    def arrived(like, sem):
        pltpu.make_async_copy(like, like, sem).wait()

    def cut(p, n):
        return pl.ds(pl.multiple_of(p * n, n), n)

    load_g = pltpu.make_async_copy(g_ref, gl, local_sem.at[0])
    load_q = pltpu.make_async_copy(q_ref, ql, local_sem.at[1])
    load_g.start()
    load_q.start()

    barrier = pltpu.get_barrier_semaphore()
    partners = z_partners + [to for pair in x_partners for to in pair] + y_partners + [sibling]
    for to in partners:
        pl.semaphore_signal(barrier, inc=1, device_id=to, device_id_type=MESH)
    pl.semaphore_wait(barrier, len(partners))

    load_g.wait()
    own_g = pltpu.make_async_copy(gl.at[:, cut(z, width)], gbuf.at[z, x, core], local_sem.at[2])
    own_g.start()
    for d, to in zip(along_z, z_partners):
        push(gl.at[:, cut(z_at(d), width)], gbuf.at[z, x, core], gz_sem.at[n_z - d], to)

    load_q.wait()
    spot = qb.at[x_lo * 2 + core]
    own_q = pltpu.make_async_copy(ql, spot, local_sem.at[3])
    own_q.start()
    near = device(x + 1 - 2 * x_lo, y, z, core), device(x + 1 - 2 * x_lo, y, z, 1 - core)
    for to in (sibling, *near):
        push(ql, spot, q_sem.at[0], to)

    own_g.wait()
    order = sorted(range(n_z), key=lambda d: ring(d, n_z))
    for d in order:
        here = gbuf.at[z_at(d), x, core]
        if d:
            arrived(here, gz_sem.at[d])
        for same, _ in x_partners:
            push(here, here, gx_sem.at[d], same)
    own_q.wait()
    arrived(qb.at[pl.ds(0, 3)], q_sem.at[0])
    qt[...] = qb[...].reshape(width, qb.shape[-1]).astype(F32).T.astype(BF16)
    for d in order:
        arrived(gbuf.at[0, pl.ds(0, NX - 1), 0], gx_sem.at[d])
        here = gbuf.at[z_at(d), :, core]
        push(here, here, gc_sem.at[d], sibling)
    query_half = qt[cut(mine, qt.shape[0] // SLICES), :]
    query = query_half.astype(F32)
    for d in order:
        arrived(gbuf.at[0, :, 0], gc_sem.at[d])

    whitened = omega * query
    carried = query_half
    for sweep in range(ITERS):
        grads = gbuf[...].reshape(n_z * SLICES * rows, width)
        part = lax.dot_general(carried, grads, (((1,), (1,)), ((), ())), preferred_element_type=F32)
        send_s[sweep] = part.astype(BF16)
        for i, to in enumerate(z_partners):
            push(send_s.at[sweep], recv_s.at[sweep, i], s_sem.at[sweep], to)
        if z_partners:
            arrived(recv_s.at[sweep], s_sem.at[sweep])
        total = send_s[sweep].astype(F32)
        for i in range(len(z_partners)):
            total = total + recv_s[sweep, i].astype(F32)

        grads = gbuf[...].reshape(n_z * SLICES * rows, width)
        part = jnp.dot(total.astype(BF16), grads, preferred_element_type=F32)
        send_t[sweep] = part.astype(BF16)
        for i, to in enumerate(y_partners):
            push(send_t.at[sweep], recv_t.at[sweep, i], t_sem.at[sweep], to)
        if y_partners:
            arrived(recv_t.at[sweep], t_sem.at[sweep])
        total = send_t[sweep].astype(F32)
        for i in range(len(y_partners)):
            total = total + recv_t[sweep, i].astype(F32)
        applied = total * (1.0 / total_rows)
        if sweep == 0:
            applied = omega * applied
        whitened = whitened + omega * (query - applied - DAMP * whitened)
        carried = whitened.astype(BF16)

    wlast[mine] = carried
    spot = wlast.at[mine]
    for pair in x_partners:
        for to in pair:
            push(spot, spot, w_sem.at[0], to)
    push(spot, spot, w_sem.at[0], sibling)
    arrived(wlast.at[pl.ds(0, SLICES - 1)], w_sem.at[0])
    queries = wlast[...].reshape(qt.shape[0], width)
    grads = gbuf[:, x, core].reshape(n_z * rows, width)
    part = lax.dot_general(grads, queries, (((1,), (1,)), ((), ())), preferred_element_type=F32)
    send_o[...] = part.reshape(send_o.shape)
    for i, (d, to) in enumerate(zip(along_z, z_partners)):
        push(send_o.at[z_at(d)], recv_o.at[i], o_sem.at[0], to)
    if z_partners:
        arrived(recv_o, o_sem.at[0])
    total = send_o[z]
    for i in range(len(z_partners)):
        total = total + recv_o[i]
    o_ref[...] = total

    for src in leaving:
        arrived(src, send_sem.at[0])


def body(n_grp, n_dev, train_grads, query_grads):
    rows, width = train_grads.shape
    block, queries = query_grads.shape
    n_z = n_dev // 4
    ny = n_grp * 2 // NX
    total_rows = rows * n_grp * n_dev
    omega = step_size(width, total_rows)
    slice_q = queries // SLICES
    held = 4 * block
    others_z, others_y = max(n_z - 1, 1), max(ny - 1, 1)
    vmem = pl.BlockSpec(memory_space=pltpu.VMEM)
    anywhere = pl.BlockSpec(memory_space=pl.ANY)
    dma = pltpu.SemaphoreType.DMA
    return pl.pallas_call(
        functools.partial(kernel, n_grp, n_z, omega, total_rows),
        name="influence",
        out_shape=jax.ShapeDtypeStruct((rows, queries), F32),
        in_specs=[anywhere, anywhere],
        out_specs=vmem,
        scratch_shapes=[
            pltpu.VMEM((rows, width), BF16),
            pltpu.VMEM((block, queries), BF16),
            pltpu.VMEM((n_z, NX, CORES, rows, held), BF16),
            pltpu.VMEM((4, block, queries), BF16),
            pltpu.VMEM((queries, held), BF16),
            pltpu.VMEM((ITERS, slice_q, n_z * SLICES * rows), BF16),
            pltpu.VMEM((ITERS, others_z, slice_q, n_z * SLICES * rows), BF16),
            pltpu.VMEM((ITERS, slice_q, held), BF16),
            pltpu.VMEM((ITERS, others_y, slice_q, held), BF16),
            pltpu.VMEM((SLICES, slice_q, held), BF16),
            pltpu.VMEM((n_z, rows, queries), F32),
            pltpu.VMEM((others_z, rows, queries), F32),
            dma((4,)), dma((1,)), dma((1,)), dma((n_z,)), dma((n_z,)), dma((n_z,)),
            dma((ITERS,)), dma((ITERS,)), dma((1,)), dma((1,)),
        ],
        compiler_params=pltpu.CompilerParams(
            collective_id=0, has_side_effects=True, vmem_limit_bytes=56 * 1024 * 1024
        ),
    )(train_grads, query_grads)


def solution(mesh):
    return jax.shard_map(
        functools.partial(body, mesh.shape["grp"], mesh.shape["dev"]),
        mesh=mesh,
        in_specs=(P(("grp", "dev"), None), P("dev", None)),
        out_specs=P(("grp", "dev"), None),
        check_vma=False,
    )
```

time: 665 us -> 65.5 us (0.10)
  waiting for transfers between devices: 618 us -> 0 us
  Pallas kernels: 0 us -> 64.1 us
  matrix products: 32.7 us -> 0 us
  between operations: 13.1 us -> 0.01 us
    psum x1 -> x0, waiting for transfers between devices: 349 us -> none  [body(): fisher_rows = lax.psum(partial_tile, 'grp') / total_rows]
    all_gather x4 -> x0, waiting for transfers between devices: 268 us -> none  [the longest x2 127 us: body(): lax.all_gather(whitened_rows, 'dev', axis=0, tiled=True)]
    pallas_call x0 -> x1, Pallas kernels: none -> 64.1 us  [body(): pl.pallas_call(functools.partial(kernel, n_grp, n_z, omega, total_rows),...]
    dot_general x4 -> x0, matrix products: 32.7 us -> none  [the longest x2 21 us: body(): jnp.dot(fisher_rows, lax.all_gather(whitened_rows, 'dev', axis=0, tiled=T...]
  transfers between devices with their start and end apart: 5 -> 0, of which waited for: 5 -> 0; matrix products, arithmetic and copies ran while one was open for 2% -> 0% of each run, Pallas kernels for 0% -> 0%
where the time goes in v3:
time: 65.5 us; the launch traced here: 65.4 us
  Pallas kernels  64.1 us (98%)
  local copies, waits for them, and re-layouts  1.3 us (2%)
    pallas_call x1, Pallas kernels, body(): pl.pallas_call(functools.partial(kernel, n_grp, n_z, omega, total_rows),...  64.1 us

profile of v3, /device:TPU:1, one launch (start us, length us, event | category | flops | bytes accessed | tf_op | source)
XLA Modules:
  0.0 65.4 jit_solution(15967260730961346147)
XLA Ops:
  0.0 64.1 %influence.1 = f32[16,128]{1,0:T(8,128)} custom-call(bf16[16,8192]{1,0:T(8,128)(2,1)} %g_ref.1, bf16[256,128]{1,0:T(8,128)(2,1)} %q_ref.1), custom_call_target="tpu_custom_call" | custom-call | tf_op jit(solution)/shard_map/influence/pallas_call | solution.py:188
  64.1 1.3 %copy.4 = f32[16,128]{1,0:T(8,128)} copy(f32[16,128]{1,0:T(8,128)} %influence.1) | data formatting | bytes 16384

commit v4 on v3

--- a/solution.py
+++ b/solution.py
@@ -31,11 +31,15 @@
     return sorted(range(1, n), key=lambda d: (-ring(d, n), d))
 
 
+def dot_t(a, b):
+    return lax.dot_general(a, b, (((1,), (1,)), ((), ())), preferred_element_type=F32)
+
+
 def kernel(
     n_grp, n_z, omega, total_rows,
     g_ref, q_ref, o_ref,
-    gl, ql, gbuf, qb, qt, send_s, recv_s, send_t, recv_t, wlast, send_o, recv_o,
-    local_sem, send_sem, q_sem, gz_sem, gx_sem, gc_sem, s_sem, t_sem, w_sem, o_sem,
+    gl, ql, gbuf, qb, qt, send_f, recv_f, sums, first, send_s, recv_s, send_t, recv_t, send_o, recv_o, last, turned,
+    local_sem, send_sem, q_sem, gz_sem, gx_sem, gc_sem, f_sem, e_sem, s_sem, t_sem, o_sem, w_sem,
 ):
     rows = g_ref.shape[0]
     block = q_ref.shape[0]
@@ -56,6 +60,12 @@
     along_z = farthest_first(n_z)
     z_partners = [device(x, y, z_at(d), core) for d in along_z]
     x_partners = [[device(lax.rem(x + d, NX), y, z, c) for c in (core, 1 - core)] for d in farthest_first(NX)]
+    slice_partners = []
+    for d in farthest_first(NX):
+        there = lax.rem(x + d, NX)
+        for c in (core, 1 - core):
+            slice_partners.append((there * CORES + c, device(there, y, z, c)))
+    slice_partners.append((x * CORES + 1 - core, device(x, y, z, 1 - core)))
     y_partners = [device(x, lax.rem(y + d, ny), z, core) for d in farthest_first(ny)]
     sibling = device(x, y, z, 1 - core)
     leaving = []
@@ -85,10 +95,10 @@
     pl.semaphore_wait(barrier, len(partners))
 
     load_g.wait()
-    own_g = pltpu.make_async_copy(gl.at[:, cut(z, width)], gbuf.at[z, x, core], local_sem.at[2])
+    own_g = pltpu.make_async_copy(gl.at[:, cut(z, width)], gbuf.at[mine, z], local_sem.at[2])
     own_g.start()
-    for d, to in zip(along_z, z_partners):
-        push(gl.at[:, cut(z_at(d), width)], gbuf.at[z, x, core], gz_sem.at[n_z - d], to)
+    for d, to in reversed(list(zip(along_z, z_partners))):
+        push(gl.at[:, cut(z_at(d), width)], gbuf.at[mine, z], gz_sem.at[n_z - d], to)
 
     load_q.wait()
     spot = qb.at[x_lo * 2 + core]
@@ -99,41 +109,59 @@
         push(ql, spot, q_sem.at[0], to)
 
     own_g.wait()
-    order = sorted(range(n_z), key=lambda d: ring(d, n_z))
+    order = [0] + along_z[::-1]
     for d in order:
-        here = gbuf.at[z_at(d), x, core]
+        here = gbuf.at[mine, z_at(d)]
         if d:
             arrived(here, gz_sem.at[d])
         for same, _ in x_partners:
             push(here, here, gx_sem.at[d], same)
-    own_q.wait()
-    arrived(qb.at[pl.ds(0, 3)], q_sem.at[0])
-    qt[...] = qb[...].reshape(width, qb.shape[-1]).astype(F32).T.astype(BF16)
+        if d == 0:
+            own_q.wait()
+            arrived(qb.at[pl.ds(0, 3)], q_sem.at[0])
+            qt[...] = qb[...].reshape(width, qb.shape[-1]).astype(F32).T.astype(BF16)
+
+    grads = gbuf[mine].reshape(n_z * rows, width)
+    send_f[...] = dot_t(qt[...], grads).astype(BF16)
+    for i, to in enumerate(z_partners):
+        push(send_f, recv_f.at[i], f_sem.at[0], to)
     for d in order:
-        arrived(gbuf.at[0, pl.ds(0, NX - 1), 0], gx_sem.at[d])
-        here = gbuf.at[z_at(d), :, core]
-        push(here, here, gc_sem.at[d], sibling)
-    query_half = qt[cut(mine, qt.shape[0] // SLICES), :]
-    query = query_half.astype(F32)
-    for d in order:
-        arrived(gbuf.at[0, :, 0], gc_sem.at[d])
-
+        arrived(gbuf.at[pl.ds(0, NX - 1), 0], gx_sem.at[d])
+        for there in range(NX):
+            here = gbuf.at[there * CORES + core, z_at(d)]
+            push(here, here, gc_sem.at[0], sibling)
+    if z_partners:
+        arrived(recv_f, f_sem.at[0])
+    total = send_f[...].astype(F32)
+    for i in range(len(z_partners)):
+        total = total + recv_f[i].astype(F32)
+    sums[...] = total.astype(BF16).reshape(sums.shape)
+    own_s = pltpu.make_async_copy(sums.at[mine], first.at[mine], local_sem.at[4])
+    own_s.start()
+    for there, to in slice_partners:
+        push(sums.at[there], first.at[mine], e_sem.at[0], to)
+    own_s.wait()
+    arrived(first.at[pl.ds(0, SLICES - 1)], e_sem.at[0])
+    carried = jnp.concatenate([first[j] for j in range(SLICES)], axis=1)
+    arrived(gbuf.at[pl.ds(0, NX)], gc_sem.at[0])
+
+    query = qt[cut(mine, qt.shape[0] // SLICES), :].astype(F32)
     whitened = omega * query
-    carried = query_half
     for sweep in range(ITERS):
-        grads = gbuf[...].reshape(n_z * SLICES * rows, width)
-        part = lax.dot_general(carried, grads, (((1,), (1,)), ((), ())), preferred_element_type=F32)
-        send_s[sweep] = part.astype(BF16)
-        for i, to in enumerate(z_partners):
-            push(send_s.at[sweep], recv_s.at[sweep, i], s_sem.at[sweep], to)
-        if z_partners:
-            arrived(recv_s.at[sweep], s_sem.at[sweep])
-        total = send_s[sweep].astype(F32)
-        for i in range(len(z_partners)):
-            total = total + recv_s[sweep, i].astype(F32)
-
-        grads = gbuf[...].reshape(n_z * SLICES * rows, width)
-        part = jnp.dot(total.astype(BF16), grads, preferred_element_type=F32)
+        if sweep:
+            grads = gbuf[...].reshape(SLICES * n_z * rows, width)
+            send_s[...] = dot_t(whitened.astype(BF16), grads).astype(BF16)
+            for i, to in enumerate(z_partners):
+                push(send_s, recv_s.at[i], s_sem.at[0], to)
+            if z_partners:
+                arrived(recv_s, s_sem.at[0])
+            total = send_s[...].astype(F32)
+            for i in range(len(z_partners)):
+                total = total + recv_s[i].astype(F32)
+            carried = total.astype(BF16)
+
+        grads = gbuf[...].reshape(SLICES * n_z * rows, width)
+        part = jnp.dot(carried, grads, preferred_element_type=F32)
         send_t[sweep] = part.astype(BF16)
         for i, to in enumerate(y_partners):
             push(send_t.at[sweep], recv_t.at[sweep, i], t_sem.at[sweep], to)
@@ -146,19 +174,11 @@
         if sweep == 0:
             applied = omega * applied
         whitened = whitened + omega * (query - applied - DAMP * whitened)
-        carried = whitened.astype(BF16)
-
-    wlast[mine] = carried
-    spot = wlast.at[mine]
-    for pair in x_partners:
-        for to in pair:
-            push(spot, spot, w_sem.at[0], to)
-    push(spot, spot, w_sem.at[0], sibling)
-    arrived(wlast.at[pl.ds(0, SLICES - 1)], w_sem.at[0])
-    queries = wlast[...].reshape(qt.shape[0], width)
-    grads = gbuf[:, x, core].reshape(n_z * rows, width)
-    part = lax.dot_general(grads, queries, (((1,), (1,)), ((), ())), preferred_element_type=F32)
-    send_o[...] = part.reshape(send_o.shape)
+
+    half = whitened.astype(BF16)
+    for there in range(n_z):
+        grads = gbuf[:, there].reshape(SLICES * rows, width)
+        send_o[there] = dot_t(half, grads)
     for i, (d, to) in enumerate(zip(along_z, z_partners)):
         push(send_o.at[z_at(d)], recv_o.at[i], o_sem.at[0], to)
     if z_partners:
@@ -166,7 +186,12 @@
     total = send_o[z]
     for i in range(len(z_partners)):
         total = total + recv_o[i]
-    o_ref[...] = total
+    last[mine] = total
+    for _, to in slice_partners:
+        push(last.at[mine], last.at[mine], w_sem.at[0], to)
+    arrived(last.at[pl.ds(0, SLICES - 1)], w_sem.at[0])
+    turned[...] = last[...].reshape(qt.shape[0], SLICES * rows).T
+    o_ref[...] = turned[cut(mine, rows), :]
 
     for src in leaving:
         arrived(src, send_sem.at[0])
@@ -194,18 +219,23 @@
         scratch_shapes=[
             pltpu.VMEM((rows, width), BF16),
             pltpu.VMEM((block, queries), BF16),
-            pltpu.VMEM((n_z, NX, CORES, rows, held), BF16),
+            pltpu.VMEM((SLICES, n_z, rows, held), BF16),
             pltpu.VMEM((4, block, queries), BF16),
             pltpu.VMEM((queries, held), BF16),
-            pltpu.VMEM((ITERS, slice_q, n_z * SLICES * rows), BF16),
-            pltpu.VMEM((ITERS, others_z, slice_q, n_z * SLICES * rows), BF16),
+            pltpu.VMEM((queries, n_z * rows), BF16),
+            pltpu.VMEM((others_z, queries, n_z * rows), BF16),
+            pltpu.VMEM((SLICES, slice_q, n_z * rows), BF16),
+            pltpu.VMEM((SLICES, slice_q, n_z * rows), BF16),
+            pltpu.VMEM((slice_q, SLICES * n_z * rows), BF16),
+            pltpu.VMEM((others_z, slice_q, SLICES * n_z * rows), BF16),
             pltpu.VMEM((ITERS, slice_q, held), BF16),
             pltpu.VMEM((ITERS, others_y, slice_q, held), BF16),
-            pltpu.VMEM((SLICES, slice_q, held), BF16),
-            pltpu.VMEM((n_z, rows, queries), F32),
-            pltpu.VMEM((others_z, rows, queries), F32),
-            dma((4,)), dma((1,)), dma((1,)), dma((n_z,)), dma((n_z,)), dma((n_z,)),
-            dma((ITERS,)), dma((ITERS,)), dma((1,)), dma((1,)),
+            pltpu.VMEM((n_z, slice_q, SLICES * rows), F32),
+            pltpu.VMEM((others_z, slice_q, SLICES * rows), F32),
+            pltpu.VMEM((SLICES, slice_q, SLICES * rows), F32),
+            pltpu.VMEM((SLICES * rows, queries), F32),
+            dma((5,)), dma((1,)), dma((1,)), dma((n_z,)), dma((n_z,)), dma((1,)),
+            dma((1,)), dma((1,)), dma((1,)), dma((ITERS,)), dma((1,)), dma((1,)),
         ],
         compiler_params=pltpu.CompilerParams(
             collective_id=0, has_side_effects=True, vmem_limit_bytes=56 * 1024 * 1024

time: 65.5 us -> 58.5 us (0.89)
  Pallas kernels: 64.1 us -> 57.1 us
    pallas_call x1, Pallas kernels: 64.1 us -> 57.1 us  [body(): pl.pallas_call(functools.partial(kernel, n_grp, n_z, omega, total_rows),...]
where the time goes in v4:
time: 58.5 us; the launch traced here: 58.4 us
  Pallas kernels  57.1 us (98%)
  local copies, waits for them, and re-layouts  1.3 us (2%)
    pallas_call x1, Pallas kernels, body(): pl.pallas_call(functools.partial(kernel, n_grp, n_z, omega, total_rows),...  57.1 us
    unnamed x1, local copies, waits for them, and re-layouts  1.3 us

profile of v4, /device:TPU:1, one launch (start us, length us, event | category | flops | bytes accessed | tf_op | source)
XLA Modules:
  0.0 58.4 jit_solution(4429928120378597763)
XLA Ops:
  0.0 57.1 %influence.1 = f32[16,128]{1,0:T(8,128)} custom-call(bf16[16,8192]{1,0:T(8,128)(2,1)} %g_ref.1, bf16[256,128]{1,0:T(8,128)(2,1)} %q_ref.1), custom_call_target="tpu_custom_call" | custom-call | tf_op jit(solution)/shard_map/influence/pallas_call | solution.py:213
  57.1 1.3 %copy.4 = f32[16,128]{1,0:T(8,128)} copy(f32[16,128]{1,0:T(8,128)} %influence.1) | data formatting | bytes 16384

commit v5 on v4

--- a/solution.py
+++ b/solution.py
@@ -38,8 +38,8 @@
 def kernel(
     n_grp, n_z, omega, total_rows,
     g_ref, q_ref, o_ref,
-    gl, ql, gbuf, qb, qt, send_f, recv_f, sums, first, send_s, recv_s, send_t, recv_t, send_o, recv_o, last, turned,
-    local_sem, send_sem, q_sem, gz_sem, gx_sem, gc_sem, f_sem, e_sem, s_sem, t_sem, o_sem, w_sem,
+    gl, ql, gbuf, qb, qt, send_f, recv_f, column, sums, first, send_s, recv_s, send_t, recv_t, send_o, recv_o, last, turned,
+    local_sem, send_sem, q_sem, gz_sem, gx_sem, gc_sem, f_sem, c_sem, e_sem, s_sem, t_sem, o_sem, w_sem,
 ):
     rows = g_ref.shape[0]
     block = q_ref.shape[0]
@@ -75,10 +75,20 @@
             src_ref=src, dst_ref=dst, send_sem=send_sem.at[0], recv_sem=sem, device_id=to, device_id_type=MESH
         )
         copy.start()
-        leaving.append(src)
+        leaving.append(math.prod(src.shape) * src.dtype.itemsize)
 
     def arrived(like, sem):
         pltpu.make_async_copy(like, like, sem).wait()
+
+    def depart():
+        left = sum(leaving)
+        leaving.clear()
+        for like in (gbuf.at[0], gbuf.at[0, 0, 0], sums.at[0]):
+            size = math.prod(like.shape) * like.dtype.itemsize
+            while left >= size:
+                arrived(like, send_sem.at[0])
+                left -= size
+        assert left == 0
 
     def cut(p, n):
         return pl.ds(pl.multiple_of(p * n, n), n)
@@ -95,10 +105,12 @@
     pl.semaphore_wait(barrier, len(partners))
 
     load_g.wait()
-    own_g = pltpu.make_async_copy(gl.at[:, cut(z, width)], gbuf.at[mine, z], local_sem.at[2])
+    own_g = pltpu.make_async_copy(gl.at[:, cut(z, width)], gbuf.at[x, core, z], local_sem.at[2])
     own_g.start()
-    for d, to in reversed(list(zip(along_z, z_partners))):
-        push(gl.at[:, cut(z_at(d), width)], gbuf.at[mine, z], gz_sem.at[n_z - d], to)
+    near_first = along_z[::-1]
+    half_way = [d for d in near_first if 2 * d == n_z]
+    for d in half_way + [d for d in near_first if 2 * d != n_z]:
+        push(gl.at[:, cut(z_at(d), width)], gbuf.at[x, core, z], gz_sem.at[n_z - d], device(x, y, z_at(d), core))
 
     load_q.wait()
     spot = qb.at[x_lo * 2 + core]
@@ -108,42 +120,58 @@
     for to in (sibling, *near):
         push(ql, spot, q_sem.at[0], to)
 
+    groups = [[0]] + [[d for d in near_first if ring(d, n_z) == far] for far in range(1, n_z // 2 + 1)]
+    if len(groups) > 3:
+        groups[-2:] = groups[:-3:-1]
     own_g.wait()
-    order = [0] + along_z[::-1]
-    for d in order:
-        here = gbuf.at[mine, z_at(d)]
-        if d:
-            arrived(here, gz_sem.at[d])
-        for same, _ in x_partners:
-            push(here, here, gx_sem.at[d], same)
-        if d == 0:
+    for group in groups:
+        for d in group:
+            here = gbuf.at[x, core, z_at(d)]
+            if d:
+                arrived(here, gz_sem.at[d])
+            for same, _ in x_partners:
+                push(here, here, gx_sem.at[d], same)
+        if group == [0]:
             own_q.wait()
             arrived(qb.at[pl.ds(0, 3)], q_sem.at[0])
-            qt[...] = qb[...].reshape(width, qb.shape[-1]).astype(F32).T.astype(BF16)
-
-    grads = gbuf[mine].reshape(n_z * rows, width)
-    send_f[...] = dot_t(qt[...], grads).astype(BF16)
-    for i, to in enumerate(z_partners):
-        push(send_f, recv_f.at[i], f_sem.at[0], to)
-    for d in order:
-        arrived(gbuf.at[pl.ds(0, NX - 1), 0], gx_sem.at[d])
-        for there in range(NX):
-            here = gbuf.at[there * CORES + core, z_at(d)]
-            push(here, here, gc_sem.at[0], sibling)
+        pieces = [gbuf[x, core, z_at(d)] for d in group]
+        pieces = pieces[0] if len(pieces) == 1 else jnp.concatenate(pieces, axis=0)
+        part = jnp.dot(pieces, qb[...].reshape(width, qb.shape[-1]), preferred_element_type=F32).astype(BF16)
+        for i, d in enumerate(group):
+            send_f[d] = part[i * rows : (i + 1) * rows]
+            if d:
+                push(send_f.at[d], recv_f.at[d - 1], f_sem.at[0], device(x, y, z_at(d), core))
+    qt[...] = qb[...].reshape(width, qb.shape[-1]).astype(F32).T.astype(BF16)
     if z_partners:
         arrived(recv_f, f_sem.at[0])
-    total = send_f[...].astype(F32)
+    total = send_f[0].astype(F32)
     for i in range(len(z_partners)):
         total = total + recv_f[i].astype(F32)
+    column[z] = total.astype(BF16)
+    for to in z_partners:
+        push(column.at[z], column.at[z], c_sem.at[0], to)
+
+    def across(groups):
+        for group in groups:
+            for d in group:
+                arrived(gbuf.at[pl.ds(0, NX - 1), 0, 0], gx_sem.at[d])
+                here = gbuf.at[:, core, z_at(d)]
+                push(here, here, gc_sem.at[0], sibling)
+
+    across(groups[:-1])
+    if z_partners:
+        arrived(column.at[pl.ds(0, n_z - 1)], c_sem.at[0])
+    total = column[...].reshape(n_z * rows, qb.shape[-1]).astype(F32).T
     sums[...] = total.astype(BF16).reshape(sums.shape)
     own_s = pltpu.make_async_copy(sums.at[mine], first.at[mine], local_sem.at[4])
     own_s.start()
     for there, to in slice_partners:
         push(sums.at[there], first.at[mine], e_sem.at[0], to)
+    across(groups[-1:])
     own_s.wait()
     arrived(first.at[pl.ds(0, SLICES - 1)], e_sem.at[0])
     carried = jnp.concatenate([first[j] for j in range(SLICES)], axis=1)
-    arrived(gbuf.at[pl.ds(0, NX)], gc_sem.at[0])
+    arrived(gbuf.at[:, 0], gc_sem.at[0])
 
     query = qt[cut(mine, qt.shape[0] // SLICES), :].astype(F32)
     whitened = omega * query
@@ -177,7 +205,7 @@
 
     half = whitened.astype(BF16)
     for there in range(n_z):
-        grads = gbuf[:, there].reshape(SLICES * rows, width)
+        grads = gbuf[:, :, there].reshape(SLICES * rows, width)
         send_o[there] = dot_t(half, grads)
     for i, (d, to) in enumerate(zip(along_z, z_partners)):
         push(send_o.at[z_at(d)], recv_o.at[i], o_sem.at[0], to)
@@ -187,14 +215,14 @@
     for i in range(len(z_partners)):
         total = total + recv_o[i]
     last[mine] = total
+    depart()
     for _, to in slice_partners:
         push(last.at[mine], last.at[mine], w_sem.at[0], to)
     arrived(last.at[pl.ds(0, SLICES - 1)], w_sem.at[0])
     turned[...] = last[...].reshape(qt.shape[0], SLICES * rows).T
     o_ref[...] = turned[cut(mine, rows), :]
 
-    for src in leaving:
-        arrived(src, send_sem.at[0])
+    depart()
 
 
 def body(n_grp, n_dev, train_grads, query_grads):
@@ -219,11 +247,12 @@
         scratch_shapes=[
             pltpu.VMEM((rows, width), BF16),
             pltpu.VMEM((block, queries), BF16),
-            pltpu.VMEM((SLICES, n_z, rows, held), BF16),
+            pltpu.VMEM((NX, CORES, n_z, rows, held), BF16),
             pltpu.VMEM((4, block, queries), BF16),
             pltpu.VMEM((queries, held), BF16),
-            pltpu.VMEM((queries, n_z * rows), BF16),
-            pltpu.VMEM((others_z, queries, n_z * rows), BF16),
+            pltpu.VMEM((n_z, rows, queries), BF16),
+            pltpu.VMEM((others_z, rows, queries), BF16),
+            pltpu.VMEM((n_z, rows, queries), BF16),
             pltpu.VMEM((SLICES, slice_q, n_z * rows), BF16),
             pltpu.VMEM((SLICES, slice_q, n_z * rows), BF16),
             pltpu.VMEM((slice_q, SLICES * n_z * rows), BF16),
@@ -235,10 +264,10 @@
             pltpu.VMEM((SLICES, slice_q, SLICES * rows), F32),
             pltpu.VMEM((SLICES * rows, queries), F32),
             dma((5,)), dma((1,)), dma((1,)), dma((n_z,)), dma((n_z,)), dma((1,)),
-            dma((1,)), dma((1,)), dma((1,)), dma((ITERS,)), dma((1,)), dma((1,)),
+            dma((1,)), dma((1,)), dma((1,)), dma((1,)), dma((ITERS,)), dma((1,)), dma((1,)),
         ],
         compiler_params=pltpu.CompilerParams(
-            collective_id=0, has_side_effects=True, vmem_limit_bytes=56 * 1024 * 1024
+            collective_id=0, has_side_effects=True, vmem_limit_bytes=55168 * 1024
         ),
     )(train_grads, query_grads)
 

time: 58.5 us -> 56.7 us (0.969)
  Pallas kernels: 57.1 us -> 56 us
  local copies, waits for them, and re-layouts: 1.3 us -> 0.6 us
    pallas_call x1, Pallas kernels: 57.1 us -> 56 us  [body(): pl.pallas_call(functools.partial(kernel, n_grp, n_z, omega, total_rows),...]
    unnamed x1, local copies, waits for them, and re-layouts: 1.3 us -> 0.6 us
where the time goes in v5:
time: 56.7 us; the launch traced here: 56.6 us
  Pallas kernels  56 us (99%)
  local copies, waits for them, and re-layouts  0.6 us (1%)
    pallas_call x1, Pallas kernels, body(): pl.pallas_call(functools.partial(kernel, n_grp, n_z, omega, total_rows),...  56 us

profile of v5, /device:TPU:1, one launch (start us, length us, event | category | flops | bytes accessed | tf_op | source)
XLA Modules:
  0.0 56.6 jit_solution(2770121511628906698)
XLA Ops:
  0.0 56.0 %influence.1 = f32[16,128]{1,0:T(8,128)S(1)} custom-call(bf16[16,8192]{1,0:T(8,128)(2,1)} %g_ref.1, bf16[256,128]{1,0:T(8,128)(2,1)} %q_ref.1), custom_call_target="tpu_custom_call" | custom-call | tf_op jit(solution)/shard_map/influence/pallas_call | solution.py:241
  56.0 0.6 %copy.4 = f32[16,128]{1,0:T(8,128)} copy(f32[16,128]{1,0:T(8,128)S(1)} %influence.1) | data formatting | bytes 16384

commit v6 on v5

--- a/solution.py
+++ b/solution.py
@@ -107,10 +107,8 @@
     load_g.wait()
     own_g = pltpu.make_async_copy(gl.at[:, cut(z, width)], gbuf.at[x, core, z], local_sem.at[2])
     own_g.start()
-    near_first = along_z[::-1]
-    half_way = [d for d in near_first if 2 * d == n_z]
-    for d in half_way + [d for d in near_first if 2 * d != n_z]:
-        push(gl.at[:, cut(z_at(d), width)], gbuf.at[x, core, z], gz_sem.at[n_z - d], device(x, y, z_at(d), core))
+    for d, to in zip(along_z, z_partners):
+        push(gl.at[:, cut(z_at(d), width)], gbuf.at[x, core, z], gz_sem.at[n_z - d], to)
 
     load_q.wait()
     spot = qb.at[x_lo * 2 + core]
@@ -120,9 +118,7 @@
     for to in (sibling, *near):
         push(ql, spot, q_sem.at[0], to)
 
-    groups = [[0]] + [[d for d in near_first if ring(d, n_z) == far] for far in range(1, n_z // 2 + 1)]
-    if len(groups) > 3:
-        groups[-2:] = groups[:-3:-1]
+    groups = [[0]] + [[d for d in along_z if ring(d, n_z) == far] for far in range(n_z // 2, 0, -1)]
     own_g.wait()
     for group in groups:
         for d in group:
@@ -175,21 +171,31 @@
 
     query = qt[cut(mine, qt.shape[0] // SLICES), :].astype(F32)
     whitened = omega * query
+    half_x, half_w = NX // 2, width // 2
     for sweep in range(ITERS):
         if sweep:
+            half = whitened.astype(BF16)
+            for k in (0, 1):
+                grads = gbuf[k * half_x : (k + 1) * half_x].reshape(half_x * CORES * n_z * rows, width)
+                send_s[k] = dot_t(half, grads).astype(BF16)
+                for i, to in enumerate(z_partners):
+                    push(send_s.at[k], recv_s.at[k, i], s_sem.at[k], to)
+            carried = []
+            for k in (0, 1):
+                if z_partners:
+                    arrived(recv_s.at[k], s_sem.at[k])
+                total = send_s[k].astype(F32)
+                for i in range(len(z_partners)):
+                    total = total + recv_s[k, i].astype(F32)
+                carried.append(total.astype(BF16))
+                if k == 0:
+                    grads = gbuf[:half_x].reshape(half_x * CORES * n_z * rows, width)
+                    part = jnp.dot(carried[0], grads, preferred_element_type=F32)
+            grads = gbuf[half_x:].reshape(half_x * CORES * n_z * rows, width)
+            part = part + jnp.dot(carried[1], grads, preferred_element_type=F32)
+        else:
             grads = gbuf[...].reshape(SLICES * n_z * rows, width)
-            send_s[...] = dot_t(whitened.astype(BF16), grads).astype(BF16)
-            for i, to in enumerate(z_partners):
-                push(send_s, recv_s.at[i], s_sem.at[0], to)
-            if z_partners:
-                arrived(recv_s, s_sem.at[0])
-            total = send_s[...].astype(F32)
-            for i in range(len(z_partners)):
-                total = total + recv_s[i].astype(F32)
-            carried = total.astype(BF16)
-
-        grads = gbuf[...].reshape(SLICES * n_z * rows, width)
-        part = jnp.dot(carried, grads, preferred_element_type=F32)
+            part = jnp.dot(carried, grads, preferred_element_type=F32)
         send_t[sweep] = part.astype(BF16)
         for i, to in enumerate(y_partners):
             push(send_t.at[sweep], recv_t.at[sweep, i], t_sem.at[sweep], to)
@@ -204,18 +210,17 @@
         whitened = whitened + omega * (query - applied - DAMP * whitened)
 
     half = whitened.astype(BF16)
-    for there in range(n_z):
-        grads = gbuf[:, :, there].reshape(SLICES * rows, width)
-        send_o[there] = dot_t(half, grads)
-    for i, (d, to) in enumerate(zip(along_z, z_partners)):
-        push(send_o.at[z_at(d)], recv_o.at[i], o_sem.at[0], to)
+    for i, d in enumerate(along_z + [0]):
+        there = z_at(d)
+        send_o[there] = dot_t(half, gbuf[:, :, there].reshape(SLICES * rows, width))
+        if d:
+            push(send_o.at[there], recv_o.at[i], o_sem.at[0], z_partners[i])
     if z_partners:
         arrived(recv_o, o_sem.at[0])
     total = send_o[z]
     for i in range(len(z_partners)):
         total = total + recv_o[i]
     last[mine] = total
-    depart()
     for _, to in slice_partners:
         push(last.at[mine], last.at[mine], w_sem.at[0], to)
     arrived(last.at[pl.ds(0, SLICES - 1)], w_sem.at[0])
@@ -255,8 +260,8 @@
             pltpu.VMEM((n_z, rows, queries), BF16),
             pltpu.VMEM((SLICES, slice_q, n_z * rows), BF16),
             pltpu.VMEM((SLICES, slice_q, n_z * rows), BF16),
-            pltpu.VMEM((slice_q, SLICES * n_z * rows), BF16),
-            pltpu.VMEM((others_z, slice_q, SLICES * n_z * rows), BF16),
+            pltpu.VMEM((2, slice_q, SLICES // 2 * n_z * rows), BF16),
+            pltpu.VMEM((2, others_z, slice_q, SLICES // 2 * n_z * rows), BF16),
             pltpu.VMEM((ITERS, slice_q, held), BF16),
             pltpu.VMEM((ITERS, others_y, slice_q, held), BF16),
             pltpu.VMEM((n_z, slice_q, SLICES * rows), F32),
@@ -264,7 +269,7 @@
             pltpu.VMEM((SLICES, slice_q, SLICES * rows), F32),
             pltpu.VMEM((SLICES * rows, queries), F32),
             dma((5,)), dma((1,)), dma((1,)), dma((n_z,)), dma((n_z,)), dma((1,)),
-            dma((1,)), dma((1,)), dma((1,)), dma((1,)), dma((ITERS,)), dma((1,)), dma((1,)),
+            dma((1,)), dma((1,)), dma((1,)), dma((2,)), dma((ITERS,)), dma((1,)), dma((1,)),
         ],
         compiler_params=pltpu.CompilerParams(
             collective_id=0, has_side_effects=True, vmem_limit_bytes=55168 * 1024

time: 56.7 us -> 55.7 us (0.982)
  Pallas kernels: 56 us -> 55 us
    pallas_call x1, Pallas kernels: 56 us -> 55 us  [body(): pl.pallas_call(functools.partial(kernel, n_grp, n_z, omega, total_rows),...]
where the time goes in v6:
time: 55.7 us; the launch traced here: 55.6 us
  Pallas kernels  55 us (99%)
  local copies, waits for them, and re-layouts  0.6 us (1%)
    pallas_call x1, Pallas kernels, body(): pl.pallas_call(functools.partial(kernel, n_grp, n_z, omega, total_rows),...  55 us

profile of v6, /device:TPU:1, one launch (start us, length us, event | category | flops | bytes accessed | tf_op | source)
XLA Modules:
  0.0 55.6 jit_solution(1945768049197361016)
XLA Ops:
  0.0 55.0 %influence.1 = f32[16,128]{1,0:T(8,128)S(1)} custom-call(bf16[16,8192]{1,0:T(8,128)(2,1)} %g_ref.1, bf16[256,128]{1,0:T(8,128)(2,1)} %q_ref.1), custom_call_target="tpu_custom_call" | custom-call | tf_op jit(solution)/shard_map/influence/pallas_call | solution.py:246
  55.0 0.6 %copy.4 = f32[16,128]{1,0:T(8,128)} copy(f32[16,128]{1,0:T(8,128)S(1)} %influence.1) | data formatting | bytes 16384

commit v7 on v6

--- a/solution.py
+++ b/solution.py
@@ -35,10 +35,20 @@
     return lax.dot_general(a, b, (((1,), (1,)), ((), ())), preferred_element_type=F32)
 
 
+def wide(value):
+    high = value.astype(BF16)
+    return jnp.concatenate([high, (value - high.astype(F32)).astype(BF16)], axis=0)
+
+
+def folded(value):
+    half = value.shape[0] // 2
+    return value[:half] + value[half:]
+
+
 def kernel(
     n_grp, n_z, omega, total_rows,
     g_ref, q_ref, o_ref,
-    gl, ql, gbuf, qb, qt, send_f, recv_f, column, sums, first, send_s, recv_s, send_t, recv_t, send_o, recv_o, last, turned,
+    gl, ql, gbuf, qb, qt, send_f, recv_f, column, sums, first, send_s, recv_s, send_t, recv_t, swap, spread, send_o, recv_o,
     local_sem, send_sem, q_sem, gz_sem, gx_sem, gc_sem, f_sem, c_sem, e_sem, s_sem, t_sem, o_sem, w_sem,
 ):
     rows = g_ref.shape[0]
@@ -171,28 +181,26 @@
 
     query = qt[cut(mine, qt.shape[0] // SLICES), :].astype(F32)
     whitened = omega * query
-    half_x, half_w = NX // 2, width // 2
+    half_x, slice_q = NX // 2, qt.shape[0] // SLICES
     for sweep in range(ITERS):
         if sweep:
-            half = whitened.astype(BF16)
+            both = wide(whitened)
+            own = []
             for k in (0, 1):
                 grads = gbuf[k * half_x : (k + 1) * half_x].reshape(half_x * CORES * n_z * rows, width)
-                send_s[k] = dot_t(half, grads).astype(BF16)
+                own.append(folded(dot_t(both, grads)))
+                send_s[k] = own[k].astype(BF16)
                 for i, to in enumerate(z_partners):
                     push(send_s.at[k], recv_s.at[k, i], s_sem.at[k], to)
-            carried = []
+            part = jnp.zeros((slice_q, width), F32)
             for k in (0, 1):
                 if z_partners:
                     arrived(recv_s.at[k], s_sem.at[k])
-                total = send_s[k].astype(F32)
+                total = own[k]
                 for i in range(len(z_partners)):
                     total = total + recv_s[k, i].astype(F32)
-                carried.append(total.astype(BF16))
-                if k == 0:
-                    grads = gbuf[:half_x].reshape(half_x * CORES * n_z * rows, width)
-                    part = jnp.dot(carried[0], grads, preferred_element_type=F32)
-            grads = gbuf[half_x:].reshape(half_x * CORES * n_z * rows, width)
-            part = part + jnp.dot(carried[1], grads, preferred_element_type=F32)
+                grads = gbuf[k * half_x : (k + 1) * half_x].reshape(half_x * CORES * n_z * rows, width)
+                part = part + folded(jnp.dot(wide(total), grads, preferred_element_type=F32))
         else:
             grads = gbuf[...].reshape(SLICES * n_z * rows, width)
             part = jnp.dot(carried, grads, preferred_element_type=F32)
@@ -201,7 +209,7 @@
             push(send_t.at[sweep], recv_t.at[sweep, i], t_sem.at[sweep], to)
         if y_partners:
             arrived(recv_t.at[sweep], t_sem.at[sweep])
-        total = send_t[sweep].astype(F32)
+        total = part
         for i in range(len(y_partners)):
             total = total + recv_t[sweep, i].astype(F32)
         applied = total * (1.0 / total_rows)
@@ -209,25 +217,38 @@
             applied = omega * applied
         whitened = whitened + omega * (query - applied - DAMP * whitened)
 
-    half = whitened.astype(BF16)
-    for i, d in enumerate(along_z + [0]):
-        there = z_at(d)
-        send_o[there] = dot_t(half, gbuf[:, :, there].reshape(SLICES * rows, width))
-        if d:
-            push(send_o.at[there], recv_o.at[i], o_sem.at[0], z_partners[i])
-    if z_partners:
-        arrived(recv_o, o_sem.at[0])
-    total = send_o[z]
-    for i in range(len(z_partners)):
-        total = total + recv_o[i]
-    last[mine] = total
-    for _, to in slice_partners:
-        push(last.at[mine], last.at[mine], w_sem.at[0], to)
-    arrived(last.at[pl.ds(0, SLICES - 1)], w_sem.at[0])
-    turned[...] = last[...].reshape(qt.shape[0], SLICES * rows).T
-    o_ref[...] = turned[cut(mine, rows), :]
-
+    swap[core] = whitened.astype(BF16)
+    push(swap.at[core], swap.at[core], w_sem.at[0], sibling)
+    spread[...] = jnp.zeros_like(spread)
+    arrived(swap.at[0], w_sem.at[0])
+    at = lax.rem(x, 2) * CORES
+    for c in range(CORES):
+        spread[cut(at + c, slice_q), :] = swap[c]
+    over_x = farthest_first(NX) + [0]
+    over_z = along_z + [0]
+    rows_h = rows // 2
+    for k, dx in enumerate(over_x):
+        there = lax.rem(x + dx, NX)
+        part = dot_t(gbuf[there, core].reshape(n_z * rows, width), spread[...]).reshape(n_z, rows, 128)
+        send_o[there] = part[:, :rows_h] + pltpu.roll(part[:, rows_h:], 64, 2)
+        for i, dz in enumerate(over_z):
+            if dx or dz:
+                to = device(there, y, z_at(dz), core)
+                push(send_o.at[there, z_at(dz)], recv_o.at[k * n_z + i], o_sem.at[0], to)
     depart()
+    arrived(recv_o.at[pl.ds(0, NX * n_z - 1)], o_sem.at[0])
+    lower = jnp.zeros((rows_h, 128), F32)
+    upper = jnp.zeros((rows_h, 128), F32)
+    for k, dx in enumerate(over_x):
+        total = send_o[x, z] if dx == 0 else recv_o[k * n_z + n_z - 1]
+        for i in range(n_z - 1):
+            total = total + recv_o[k * n_z + i]
+        source = lax.rem(x + NX - dx, NX)
+        lower = lower + jnp.where(source < 2, total, 0.0)
+        upper = upper + jnp.where(source < 2, 0.0, total)
+    left = lax.broadcasted_iota(jnp.int32, lower.shape, 1) < 64
+    o_ref[0:rows_h, :] = jnp.where(left, lower, pltpu.roll(upper, 64, 1))
+    o_ref[rows_h:rows, :] = jnp.where(left, pltpu.roll(lower, 64, 1), upper)
 
 
 def body(n_grp, n_dev, train_grads, query_grads):
@@ -264,10 +285,10 @@
             pltpu.VMEM((2, others_z, slice_q, SLICES // 2 * n_z * rows), BF16),
             pltpu.VMEM((ITERS, slice_q, held), BF16),
             pltpu.VMEM((ITERS, others_y, slice_q, held), BF16),
-            pltpu.VMEM((n_z, slice_q, SLICES * rows), F32),
-            pltpu.VMEM((others_z, slice_q, SLICES * rows), F32),
-            pltpu.VMEM((SLICES, slice_q, SLICES * rows), F32),
-            pltpu.VMEM((SLICES * rows, queries), F32),
+            pltpu.VMEM((CORES, slice_q, held), BF16),
+            pltpu.VMEM((queries, held), BF16),
+            pltpu.VMEM((NX, n_z, rows // 2, queries), F32),
+            pltpu.VMEM((NX * n_z, rows // 2, queries), F32),
             dma((5,)), dma((1,)), dma((1,)), dma((n_z,)), dma((n_z,)), dma((1,)),
             dma((1,)), dma((1,)), dma((1,)), dma((2,)), dma((ITERS,)), dma((1,)), dma((1,)),
         ],

time: 55.7 us -> 54.3 us (0.975)
  Pallas kernels: 55 us -> 53.6 us
    pallas_call x1, Pallas kernels: 55 us -> 53.6 us  [body(): pl.pallas_call(functools.partial(kernel, n_grp, n_z, omega, total_rows),...]
where the time goes in v7:
time: 54.3 us; the launch traced here: 54.2 us
  Pallas kernels  53.6 us (99%)
  local copies, waits for them, and re-layouts  0.6 us (1%)
    pallas_call x1, Pallas kernels, body(): pl.pallas_call(functools.partial(kernel, n_grp, n_z, omega, total_rows),...  53.6 us

profile of v7, /device:TPU:1, one launch (start us, length us, event | category | flops | bytes accessed | tf_op | source)
XLA Modules:
  0.0 54.2 jit_solution(3451947214294419328)
XLA Ops:
  0.0 53.6 %influence.1 = f32[16,128]{1,0:T(8,128)S(1)} custom-call(bf16[16,8192]{1,0:T(8,128)(2,1)} %g_ref.1, bf16[256,128]{1,0:T(8,128)(2,1)} %q_ref.1), custom_call_target="tpu_custom_call" | custom-call | tf_op jit(solution)/shard_map/influence/pallas_call | solution.py:267
  53.6 0.6 %copy.4 = f32[16,128]{1,0:T(8,128)} copy(f32[16,128]{1,0:T(8,128)S(1)} %influence.1) | data formatting | bytes 16384

commit v8 on v7

--- a/solution.py
+++ b/solution.py
@@ -48,8 +48,8 @@
 def kernel(
     n_grp, n_z, omega, total_rows,
     g_ref, q_ref, o_ref,
-    gl, ql, gbuf, qb, qt, send_f, recv_f, column, sums, first, send_s, recv_s, send_t, recv_t, swap, spread, send_o, recv_o,
-    local_sem, send_sem, q_sem, gz_sem, gx_sem, gc_sem, f_sem, c_sem, e_sem, s_sem, t_sem, o_sem, w_sem,
+    gl, ql, gbuf, qb, qt, send_f, recv_f, column, sums, recv_e, first, send_s, recv_s, send_t, recv_t, cross_t, swap, spread, send_o, recv_o,
+    local_sem, send_sem, q_sem, gz_sem, gx_sem, gc_sem, f_sem, ready_sem, e_sem, s_sem, t_sem, o_sem, w_sem,
 ):
     rows = g_ref.shape[0]
     block = q_ref.shape[0]
@@ -69,15 +69,11 @@
 
     along_z = farthest_first(n_z)
     z_partners = [device(x, y, z_at(d), core) for d in along_z]
+    z_crossed = [device(x, y, z_at(d), 1 - core) for d in along_z]
     x_partners = [[device(lax.rem(x + d, NX), y, z, c) for c in (core, 1 - core)] for d in farthest_first(NX)]
-    slice_partners = []
-    for d in farthest_first(NX):
-        there = lax.rem(x + d, NX)
-        for c in (core, 1 - core):
-            slice_partners.append((there * CORES + c, device(there, y, z, c)))
-    slice_partners.append((x * CORES + 1 - core, device(x, y, z, 1 - core)))
     y_partners = [device(x, lax.rem(y + d, ny), z, core) for d in farthest_first(ny)]
     sibling = device(x, y, z, 1 - core)
+    y_crossed = [device(x, lax.rem(y + d, ny), z, 1 - core) for d in farthest_first(ny)]
     leaving = []
 
     def push(src, dst, sem, to):
@@ -109,7 +105,7 @@
     load_q.start()
 
     barrier = pltpu.get_barrier_semaphore()
-    partners = z_partners + [to for pair in x_partners for to in pair] + y_partners + [sibling]
+    partners = z_partners + z_crossed + [to for pair in x_partners for to in pair] + y_partners + [sibling]
     for to in partners:
         pl.semaphore_signal(barrier, inc=1, device_id=to, device_id_type=MESH)
     pl.semaphore_wait(barrier, len(partners))
@@ -117,8 +113,12 @@
     load_g.wait()
     own_g = pltpu.make_async_copy(gl.at[:, cut(z, width)], gbuf.at[x, core, z], local_sem.at[2])
     own_g.start()
-    for d, to in zip(along_z, z_partners):
-        push(gl.at[:, cut(z_at(d), width)], gbuf.at[x, core, z], gz_sem.at[n_z - d], to)
+    groups = [[0]] + [[d for d in along_z if ring(d, n_z) == far] for far in range(n_z // 2, 0, -1)]
+    if len(groups) > 2:
+        groups.insert(1, groups.pop())
+    for group in groups[1:]:
+        for d in group:
+            push(gl.at[:, cut(z_at(d), width)], gbuf.at[x, core, z], gz_sem.at[n_z - d], device(x, y, z_at(d), core))
 
     load_q.wait()
     spot = qb.at[x_lo * 2 + core]
@@ -128,7 +128,13 @@
     for to in (sibling, *near):
         push(ql, spot, q_sem.at[0], to)
 
-    groups = [[0]] + [[d for d in along_z if ring(d, n_z) == far] for far in range(n_z // 2, 0, -1)]
+    def across(groups):
+        for group in groups:
+            for d in group:
+                arrived(gbuf.at[pl.ds(0, NX - 1), 0, 0], gx_sem.at[d])
+                here = gbuf.at[:, core, z_at(d)]
+                push(here, here, gc_sem.at[0], sibling)
+
     own_g.wait()
     for group in groups:
         for d in group:
@@ -146,37 +152,46 @@
         for i, d in enumerate(group):
             send_f[d] = part[i * rows : (i + 1) * rows]
             if d:
-                push(send_f.at[d], recv_f.at[d - 1], f_sem.at[0], device(x, y, z_at(d), core))
+                push(send_f.at[d], recv_f.at[0, d], f_sem.at[0], device(x, y, z_at(d), core))
+                push(send_f.at[d], recv_f.at[1, d], f_sem.at[1], device(x, y, z_at(d), 1 - core))
+            else:
+                push(send_f.at[d], recv_f.at[1, d], f_sem.at[1], sibling)
+
+    over_x = farthest_first(NX) + [0]
+    over_z = along_z + [0]
+    for same, _ in x_partners:
+        pl.semaphore_signal(ready_sem, inc=1, device_id=same, device_id_type=MESH)
     qt[...] = qb[...].reshape(width, qb.shape[-1]).astype(F32).T.astype(BF16)
+    column[...] = jnp.zeros_like(column)
+    spread[...] = jnp.zeros_like(spread)
+    across(groups[:3])
+    arrived(recv_f.at[1], f_sem.at[1])
     if z_partners:
-        arrived(recv_f, f_sem.at[0])
+        arrived(recv_f.at[0, pl.ds(0, n_z - 1)], f_sem.at[0])
     total = send_f[0].astype(F32)
-    for i in range(len(z_partners)):
-        total = total + recv_f[i].astype(F32)
-    column[z] = total.astype(BF16)
-    for to in z_partners:
-        push(column.at[z], column.at[z], c_sem.at[0], to)
-
-    def across(groups):
-        for group in groups:
-            for d in group:
-                arrived(gbuf.at[pl.ds(0, NX - 1), 0, 0], gx_sem.at[d])
-                here = gbuf.at[:, core, z_at(d)]
-                push(here, here, gc_sem.at[0], sibling)
-
-    across(groups[:-1])
-    if z_partners:
-        arrived(column.at[pl.ds(0, n_z - 1)], c_sem.at[0])
-    total = column[...].reshape(n_z * rows, qb.shape[-1]).astype(F32).T
-    sums[...] = total.astype(BF16).reshape(sums.shape)
-    own_s = pltpu.make_async_copy(sums.at[mine], first.at[mine], local_sem.at[4])
-    own_s.start()
-    for there, to in slice_partners:
-        push(sums.at[there], first.at[mine], e_sem.at[0], to)
-    across(groups[-1:])
-    own_s.wait()
-    arrived(first.at[pl.ds(0, SLICES - 1)], e_sem.at[0])
-    carried = jnp.concatenate([first[j] for j in range(SLICES)], axis=1)
+    for d in range(1, n_z):
+        total = total + recv_f[0, d].astype(F32)
+    column[cut(mine, rows), :] = total
+    total = recv_f[1, 0].astype(F32)
+    for d in range(1, n_z):
+        total = total + recv_f[1, d].astype(F32)
+    column[cut(x * CORES + 1 - core, rows), :] = total
+    sums[...] = column[...].T.astype(BF16).reshape(sums.shape)
+    pl.semaphore_wait(ready_sem, NX - 1)
+    for k, dx in enumerate(over_x):
+        there = lax.rem(x + dx, NX)
+        for i, dz in enumerate(over_z):
+            if dx or dz:
+                to = device(there, y, z_at(dz), core)
+                push(sums.at[there * CORES + core], recv_e.at[k * n_z + i], e_sem.at[0], to)
+    across(groups[3:])
+    arrived(recv_e.at[pl.ds(0, NX * n_z - 1)], e_sem.at[0])
+    for i, dz in enumerate(over_z):
+        total = sums[mine] if dz == 0 else recv_e[(NX - 1) * n_z + i]
+        for k in range(NX - 1):
+            total = total + recv_e[k * n_z + i]
+        first[z_at(n_z - dz)] = total
+    carried = jnp.concatenate([first[there] for there in range(n_z)], axis=1)
     arrived(gbuf.at[:, 0], gc_sem.at[0])
 
     query = qt[cut(mine, qt.shape[0] // SLICES), :].astype(F32)
@@ -202,9 +217,12 @@
                 grads = gbuf[k * half_x : (k + 1) * half_x].reshape(half_x * CORES * n_z * rows, width)
                 part = part + folded(jnp.dot(wide(total), grads, preferred_element_type=F32))
         else:
-            grads = gbuf[...].reshape(SLICES * n_z * rows, width)
-            part = jnp.dot(carried, grads, preferred_element_type=F32)
+            grads = [gbuf[:, :, there].reshape(SLICES * rows, width) for there in range(n_z)]
+            part = jnp.dot(carried, jnp.concatenate(grads, axis=0), preferred_element_type=F32)
         send_t[sweep] = part.astype(BF16)
+        if sweep == ITERS - 1:
+            for i, to in enumerate(y_crossed + [sibling]):
+                push(send_t.at[sweep], cross_t.at[i], w_sem.at[1], to)
         for i, to in enumerate(y_partners):
             push(send_t.at[sweep], recv_t.at[sweep, i], t_sem.at[sweep], to)
         if y_partners:
@@ -216,16 +234,23 @@
         if sweep == 0:
             applied = omega * applied
         whitened = whitened + omega * (query - applied - DAMP * whitened)
-
-    swap[core] = whitened.astype(BF16)
-    push(swap.at[core], swap.at[core], w_sem.at[0], sibling)
-    spread[...] = jnp.zeros_like(spread)
+        if sweep == ITERS - 2:
+            swap[core] = whitened
+            push(swap.at[core], swap.at[core], w_sem.at[0], sibling)
+
+    other = x * CORES + 1 - core
     arrived(swap.at[0], w_sem.at[0])
+    arrived(cross_t, w_sem.at[1])
+    total = cross_t[0].astype(F32)
+    for i in range(1, ny):
+        total = total + cross_t[i].astype(F32)
+    crossed = swap[1 - core]
+    query = qt[cut(other, slice_q), :].astype(F32)
+    crossed = crossed + omega * (query - total * (1.0 / total_rows) - DAMP * crossed)
+
     at = lax.rem(x, 2) * CORES
-    for c in range(CORES):
-        spread[cut(at + c, slice_q), :] = swap[c]
-    over_x = farthest_first(NX) + [0]
-    over_z = along_z + [0]
+    spread[cut(at + core, slice_q), :] = whitened.astype(BF16)
+    spread[cut(at + 1 - core, slice_q), :] = crossed.astype(BF16)
     rows_h = rows // 2
     for k, dx in enumerate(over_x):
         there = lax.rem(x + dx, NX)
@@ -277,20 +302,22 @@
             pltpu.VMEM((4, block, queries), BF16),
             pltpu.VMEM((queries, held), BF16),
             pltpu.VMEM((n_z, rows, queries), BF16),
-            pltpu.VMEM((others_z, rows, queries), BF16),
-            pltpu.VMEM((n_z, rows, queries), BF16),
-            pltpu.VMEM((SLICES, slice_q, n_z * rows), BF16),
-            pltpu.VMEM((SLICES, slice_q, n_z * rows), BF16),
+            pltpu.VMEM((CORES, n_z, rows, queries), BF16),
+            pltpu.VMEM((SLICES * rows, queries), F32),
+            pltpu.VMEM((SLICES, slice_q, SLICES * rows), BF16),
+            pltpu.VMEM((NX * n_z, slice_q, SLICES * rows), BF16),
+            pltpu.VMEM((n_z, slice_q, SLICES * rows), BF16),
             pltpu.VMEM((2, slice_q, SLICES // 2 * n_z * rows), BF16),
             pltpu.VMEM((2, others_z, slice_q, SLICES // 2 * n_z * rows), BF16),
             pltpu.VMEM((ITERS, slice_q, held), BF16),
             pltpu.VMEM((ITERS, others_y, slice_q, held), BF16),
-            pltpu.VMEM((CORES, slice_q, held), BF16),
+            pltpu.VMEM((ny, slice_q, held), BF16),
+            pltpu.VMEM((CORES, slice_q, held), F32),
             pltpu.VMEM((queries, held), BF16),
             pltpu.VMEM((NX, n_z, rows // 2, queries), F32),
             pltpu.VMEM((NX * n_z, rows // 2, queries), F32),
             dma((5,)), dma((1,)), dma((1,)), dma((n_z,)), dma((n_z,)), dma((1,)),
-            dma((1,)), dma((1,)), dma((1,)), dma((2,)), dma((ITERS,)), dma((1,)), dma((1,)),
+            dma((2,)), pltpu.SemaphoreType.REGULAR, dma((1,)), dma((2,)), dma((ITERS,)), dma((1,)), dma((2,)),
         ],
         compiler_params=pltpu.CompilerParams(
             collective_id=0, has_side_effects=True, vmem_limit_bytes=55168 * 1024

time: 54.3 us -> 53 us (0.976)
  Pallas kernels: 53.6 us -> 52.2 us
    pallas_call x1, Pallas kernels: 53.6 us -> 52.2 us  [body(): pl.pallas_call(functools.partial(kernel, n_grp, n_z, omega, total_rows),...]
where the time goes in v8:
time: 53 us; the launch traced here: 52.8 us
  Pallas kernels  52.2 us (98%)
  local copies, waits for them, and re-layouts  0.6 us (1%)
    pallas_call x1, Pallas kernels, body(): pl.pallas_call(functools.partial(kernel, n_grp, n_z, omega, total_rows),...  52.2 us

profile of v8, /device:TPU:1, one launch (start us, length us, event | category | flops | bytes accessed | tf_op | source)
XLA Modules:
  0.0 52.8 jit_solution(12292570569639762899)
XLA Ops:
  0.0 52.2 %influence.1 = f32[16,128]{1,0:T(8,128)S(1)} custom-call(bf16[16,8192]{1,0:T(8,128)(2,1)} %g_ref.1, bf16[256,128]{1,0:T(8,128)(2,1)} %q_ref.1), custom_call_target="tpu_custom_call" | custom-call | tf_op jit(solution)/shard_map/influence/pallas_call | solution.py:292
  52.2 0.6 %copy.4 = f32[16,128]{1,0:T(8,128)} copy(f32[16,128]{1,0:T(8,128)S(1)} %influence.1) | data formatting | bytes 16384

commit v9 on v8

--- a/solution.py
+++ b/solution.py
@@ -114,11 +114,12 @@
     own_g = pltpu.make_async_copy(gl.at[:, cut(z, width)], gbuf.at[x, core, z], local_sem.at[2])
     own_g.start()
     groups = [[0]] + [[d for d in along_z if ring(d, n_z) == far] for far in range(n_z // 2, 0, -1)]
-    if len(groups) > 2:
-        groups.insert(1, groups.pop())
-    for group in groups[1:]:
+    if len(groups) > 1:
+        groups[0] = groups[0] + groups.pop()
+    for group in groups:
         for d in group:
-            push(gl.at[:, cut(z_at(d), width)], gbuf.at[x, core, z], gz_sem.at[n_z - d], device(x, y, z_at(d), core))
+            if d:
+                push(gl.at[:, cut(z_at(d), width)], gbuf.at[x, core, z], gz_sem.at[n_z - d], device(x, y, z_at(d), core))
 
     load_q.wait()
     spot = qb.at[x_lo * 2 + core]
@@ -143,7 +144,7 @@
                 arrived(here, gz_sem.at[d])
             for same, _ in x_partners:
                 push(here, here, gx_sem.at[d], same)
-        if group == [0]:
+        if 0 in group:
             own_q.wait()
             arrived(qb.at[pl.ds(0, 3)], q_sem.at[0])
         pieces = [gbuf[x, core, z_at(d)] for d in group]
@@ -159,12 +160,14 @@
 
     over_x = farthest_first(NX) + [0]
     over_z = along_z + [0]
+    far = {(k, i): ring(dx, NX) + ring(dz, n_z) for k, dx in enumerate(over_x) for i, dz in enumerate(over_z)}
+    by_distance = sorted((pair for pair in far if far[pair]), key=lambda pair: -far[pair])
     for same, _ in x_partners:
         pl.semaphore_signal(ready_sem, inc=1, device_id=same, device_id_type=MESH)
     qt[...] = qb[...].reshape(width, qb.shape[-1]).astype(F32).T.astype(BF16)
     column[...] = jnp.zeros_like(column)
     spread[...] = jnp.zeros_like(spread)
-    across(groups[:3])
+    across(groups[:2])
     arrived(recv_f.at[1], f_sem.at[1])
     if z_partners:
         arrived(recv_f.at[0, pl.ds(0, n_z - 1)], f_sem.at[0])
@@ -178,13 +181,11 @@
     column[cut(x * CORES + 1 - core, rows), :] = total
     sums[...] = column[...].T.astype(BF16).reshape(sums.shape)
     pl.semaphore_wait(ready_sem, NX - 1)
-    for k, dx in enumerate(over_x):
-        there = lax.rem(x + dx, NX)
-        for i, dz in enumerate(over_z):
-            if dx or dz:
-                to = device(there, y, z_at(dz), core)
-                push(sums.at[there * CORES + core], recv_e.at[k * n_z + i], e_sem.at[0], to)
-    across(groups[3:])
+    for k, i in by_distance:
+        there = lax.rem(x + over_x[k], NX)
+        to = device(there, y, z_at(over_z[i]), core)
+        push(sums.at[there * CORES + core], recv_e.at[k * n_z + i], e_sem.at[0], to)
+    across(groups[2:])
     arrived(recv_e.at[pl.ds(0, NX * n_z - 1)], e_sem.at[0])
     for i, dz in enumerate(over_z):
         total = sums[mine] if dz == 0 else recv_e[(NX - 1) * n_z + i]
@@ -252,14 +253,22 @@
     spread[cut(at + core, slice_q), :] = whitened.astype(BF16)
     spread[cut(at + 1 - core, slice_q), :] = crossed.astype(BF16)
     rows_h = rows // 2
+
+    def put(pair):
+        k, i = pair
+        there, z_there = lax.rem(x + over_x[k], NX), z_at(over_z[i])
+        push(send_o.at[there, z_there], recv_o.at[k * n_z + i], o_sem.at[0], device(there, y, z_there, core))
+
     for k, dx in enumerate(over_x):
         there = lax.rem(x + dx, NX)
         part = dot_t(gbuf[there, core].reshape(n_z * rows, width), spread[...]).reshape(n_z, rows, 128)
         send_o[there] = part[:, :rows_h] + pltpu.roll(part[:, rows_h:], 64, 2)
-        for i, dz in enumerate(over_z):
-            if dx or dz:
-                to = device(there, y, z_at(dz), core)
-                push(send_o.at[there, z_at(dz)], recv_o.at[k * n_z + i], o_sem.at[0], to)
+        for pair in by_distance:
+            if pair[0] == k and far[pair] >= 4:
+                put(pair)
+    for pair in by_distance:
+        if far[pair] < 4:
+            put(pair)
     depart()
     arrived(recv_o.at[pl.ds(0, NX * n_z - 1)], o_sem.at[0])
     lower = jnp.zeros((rows_h, 128), F32)

time: 53 us -> 52.3 us (0.987)
  Pallas kernels: 52.2 us -> 51.4 us
    pallas_call x1, Pallas kernels: 52.2 us -> 51.4 us  [body(): pl.pallas_call(functools.partial(kernel, n_grp, n_z, omega, total_rows),...]
where the time goes in v9:
time: 52.3 us; the launch traced here: 52 us
  Pallas kernels  51.4 us (98%)
  local copies, waits for them, and re-layouts  0.6 us (1%)
    pallas_call x1, Pallas kernels, body(): pl.pallas_call(functools.partial(kernel, n_grp, n_z, omega, total_rows),...  51.4 us

profile of v9, /device:TPU:1, one launch (start us, length us, event | category | flops | bytes accessed | tf_op | source)
XLA Modules:
  0.0 52.0 jit_solution(1670838463260347597)
XLA Ops:
  0.0 51.4 %influence.1 = f32[16,128]{1,0:T(8,128)S(1)} custom-call(bf16[16,8192]{1,0:T(8,128)(2,1)} %g_ref.1, bf16[256,128]{1,0:T(8,128)(2,1)} %q_ref.1), custom_call_target="tpu_custom_call" | custom-call | tf_op jit(solution)/shard_map/influence/pallas_call | solution.py:301
  51.4 0.6 %copy.4 = f32[16,128]{1,0:T(8,128)} copy(f32[16,128]{1,0:T(8,128)S(1)} %influence.1) | data formatting | bytes 16384

commit v10 on v9

--- a/solution.py
+++ b/solution.py
@@ -74,6 +74,7 @@
     y_partners = [device(x, lax.rem(y + d, ny), z, core) for d in farthest_first(ny)]
     sibling = device(x, y, z, 1 - core)
     y_crossed = [device(x, lax.rem(y + d, ny), z, 1 - core) for d in farthest_first(ny)]
+    near = device(x + 1 - 2 * x_lo, y, z, core), device(x + 1 - 2 * x_lo, y, z, 1 - core)
     leaving = []
 
     def push(src, dst, sem, to):
@@ -105,7 +106,7 @@
     load_q.start()
 
     barrier = pltpu.get_barrier_semaphore()
-    partners = z_partners + z_crossed + [to for pair in x_partners for to in pair] + y_partners + [sibling]
+    partners = z_crossed + z_partners + [same for same, _ in x_partners] + [near[1]] + y_partners + [sibling]
     for to in partners:
         pl.semaphore_signal(barrier, inc=1, device_id=to, device_id_type=MESH)
     pl.semaphore_wait(barrier, len(partners))
@@ -125,7 +126,6 @@
     spot = qb.at[x_lo * 2 + core]
     own_q = pltpu.make_async_copy(ql, spot, local_sem.at[3])
     own_q.start()
-    near = device(x + 1 - 2 * x_lo, y, z, core), device(x + 1 - 2 * x_lo, y, z, 1 - core)
     for to in (sibling, *near):
         push(ql, spot, q_sem.at[0], to)
 
@@ -134,7 +134,7 @@
             for d in group:
                 arrived(gbuf.at[pl.ds(0, NX - 1), 0, 0], gx_sem.at[d])
                 here = gbuf.at[:, core, z_at(d)]
-                push(here, here, gc_sem.at[0], sibling)
+                push(here, here, gc_sem.at[d], sibling)
 
     own_g.wait()
     for group in groups:
@@ -192,9 +192,6 @@
         for k in range(NX - 1):
             total = total + recv_e[k * n_z + i]
         first[z_at(n_z - dz)] = total
-    carried = jnp.concatenate([first[there] for there in range(n_z)], axis=1)
-    arrived(gbuf.at[:, 0], gc_sem.at[0])
-
     query = qt[cut(mine, qt.shape[0] // SLICES), :].astype(F32)
     whitened = omega * query
     half_x, slice_q = NX // 2, qt.shape[0] // SLICES
@@ -218,8 +215,16 @@
                 grads = gbuf[k * half_x : (k + 1) * half_x].reshape(half_x * CORES * n_z * rows, width)
                 part = part + folded(jnp.dot(wide(total), grads, preferred_element_type=F32))
         else:
-            grads = [gbuf[:, :, there].reshape(SLICES * rows, width) for there in range(n_z)]
-            part = jnp.dot(carried, jnp.concatenate(grads, axis=0), preferred_element_type=F32)
+            part = jnp.zeros((slice_q, width), F32)
+            for some in (groups[:2], groups[2:]):
+                there = [z_at(d) for group in some for d in group]
+                for group in some:
+                    for d in group:
+                        arrived(gbuf.at[:, 0, 0], gc_sem.at[d])
+                if there:
+                    carried = jnp.concatenate([first[at] for at in there], axis=1)
+                    grads = [gbuf[:, :, at].reshape(SLICES * rows, width) for at in there]
+                    part = part + jnp.dot(carried, jnp.concatenate(grads, axis=0), preferred_element_type=F32)
         send_t[sweep] = part.astype(BF16)
         if sweep == ITERS - 1:
             for i, to in enumerate(y_crossed + [sibling]):
@@ -325,7 +330,7 @@
             pltpu.VMEM((queries, held), BF16),
             pltpu.VMEM((NX, n_z, rows // 2, queries), F32),
             pltpu.VMEM((NX * n_z, rows // 2, queries), F32),
-            dma((5,)), dma((1,)), dma((1,)), dma((n_z,)), dma((n_z,)), dma((1,)),
+            dma((5,)), dma((1,)), dma((1,)), dma((n_z,)), dma((n_z,)), dma((n_z,)),
             dma((2,)), pltpu.SemaphoreType.REGULAR, dma((1,)), dma((2,)), dma((ITERS,)), dma((1,)), dma((2,)),
         ],
         compiler_params=pltpu.CompilerParams(

time: 52.3 us -> 51.8 us (level)
  no operation moved by 1% of the time
where the time goes in v10:
time: 51.8 us; the launch traced here: 51.7 us
  Pallas kernels  51.1 us (99%)
  local copies, waits for them, and re-layouts  0.6 us (1%)
    pallas_call x1, Pallas kernels, body(): pl.pallas_call(functools.partial(kernel, n_grp, n_z, omega, total_rows),...  51.1 us

profile of v10, /device:TPU:1, one launch (start us, length us, event | category | flops | bytes accessed | tf_op | source)
XLA Modules:
  0.0 51.7 jit_solution(625879219708172000)
XLA Ops:
  0.0 51.1 %influence.1 = f32[16,128]{1,0:T(8,128)S(1)} custom-call(bf16[16,8192]{1,0:T(8,128)(2,1)} %g_ref.1, bf16[256,128]{1,0:T(8,128)(2,1)} %q_ref.1), custom_call_target="tpu_custom_call" | custom-call | tf_op jit(solution)/shard_map/influence/pallas_call | solution.py:306
  51.1 0.6 %copy.4 = f32[16,128]{1,0:T(8,128)} copy(f32[16,128]{1,0:T(8,128)S(1)} %influence.1) | data formatting | bytes 16384

commit v11 on v10

--- a/solution.py
+++ b/solution.py
@@ -74,7 +74,7 @@
     y_partners = [device(x, lax.rem(y + d, ny), z, core) for d in farthest_first(ny)]
     sibling = device(x, y, z, 1 - core)
     y_crossed = [device(x, lax.rem(y + d, ny), z, 1 - core) for d in farthest_first(ny)]
-    near = device(x + 1 - 2 * x_lo, y, z, core), device(x + 1 - 2 * x_lo, y, z, 1 - core)
+    near = device(x + 1 - 2 * x_lo, y, z, core)
     leaving = []
 
     def push(src, dst, sem, to):
@@ -106,7 +106,7 @@
     load_q.start()
 
     barrier = pltpu.get_barrier_semaphore()
-    partners = z_crossed + z_partners + [same for same, _ in x_partners] + [near[1]] + y_partners + [sibling]
+    partners = z_crossed + z_partners + [same for same, _ in x_partners] + y_partners + [sibling]
     for to in partners:
         pl.semaphore_signal(barrier, inc=1, device_id=to, device_id_type=MESH)
     pl.semaphore_wait(barrier, len(partners))
@@ -126,8 +126,8 @@
     spot = qb.at[x_lo * 2 + core]
     own_q = pltpu.make_async_copy(ql, spot, local_sem.at[3])
     own_q.start()
-    for to in (sibling, *near):
-        push(ql, spot, q_sem.at[0], to)
+    push(ql, spot, q_sem.at[0], near)
+    push(ql, spot, q_sem.at[1], sibling)
 
     def across(groups):
         for group in groups:
@@ -146,7 +146,11 @@
                 push(here, here, gx_sem.at[d], same)
         if 0 in group:
             own_q.wait()
-            arrived(qb.at[pl.ds(0, 3)], q_sem.at[0])
+            spot = qb.at[(1 - x_lo) * 2 + core]
+            arrived(spot, q_sem.at[0])
+            push(spot, spot, q_sem.at[2], sibling)
+            arrived(spot, q_sem.at[1])
+            arrived(spot, q_sem.at[2])
         pieces = [gbuf[x, core, z_at(d)] for d in group]
         pieces = pieces[0] if len(pieces) == 1 else jnp.concatenate(pieces, axis=0)
         part = jnp.dot(pieces, qb[...].reshape(width, qb.shape[-1]), preferred_element_type=F32).astype(BF16)
@@ -330,7 +334,7 @@
             pltpu.VMEM((queries, held), BF16),
             pltpu.VMEM((NX, n_z, rows // 2, queries), F32),
             pltpu.VMEM((NX * n_z, rows // 2, queries), F32),
-            dma((5,)), dma((1,)), dma((1,)), dma((n_z,)), dma((n_z,)), dma((n_z,)),
+            dma((5,)), dma((1,)), dma((3,)), dma((n_z,)), dma((n_z,)), dma((n_z,)),
             dma((2,)), pltpu.SemaphoreType.REGULAR, dma((1,)), dma((2,)), dma((ITERS,)), dma((1,)), dma((2,)),
         ],
         compiler_params=pltpu.CompilerParams(

time: 51.8 us -> 51.2 us (0.988)
  Pallas kernels: 51.1 us -> 50.4 us
    pallas_call x1, Pallas kernels: 51.1 us -> 50.4 us  [body(): pl.pallas_call(functools.partial(kernel, n_grp, n_z, omega, total_rows),...]
where the time goes in v11:
time: 51.2 us; the launch traced here: 51 us
  Pallas kernels  50.4 us (98%)
  local copies, waits for them, and re-layouts  0.6 us (1%)
    pallas_call x1, Pallas kernels, body(): pl.pallas_call(functools.partial(kernel, n_grp, n_z, omega, total_rows),...  50.4 us

profile of v11, /device:TPU:1, one launch (start us, length us, event | category | flops | bytes accessed | tf_op | source)
XLA Modules:
  0.0 51.0 jit_solution(9107230360005481789)
XLA Ops:
  0.0 50.4 %influence.1 = f32[16,128]{1,0:T(8,128)S(1)} custom-call(bf16[16,8192]{1,0:T(8,128)(2,1)} %g_ref.1, bf16[256,128]{1,0:T(8,128)(2,1)} %q_ref.1), custom_call_target="tpu_custom_call" | custom-call | tf_op jit(solution)/shard_map/influence/pallas_call | solution.py:310
  50.4 0.6 %copy.4 = f32[16,128]{1,0:T(8,128)} copy(f32[16,128]{1,0:T(8,128)S(1)} %influence.1) | data formatting | bytes 16384

commit v12 on v11

--- a/solution.py
+++ b/solution.py
@@ -209,6 +209,8 @@
                 send_s[k] = own[k].astype(BF16)
                 for i, to in enumerate(z_partners):
                     push(send_s.at[k], recv_s.at[k, i], s_sem.at[k], to)
+            swap[core] = whitened
+            push(swap.at[core], swap.at[core], w_sem.at[0], sibling)
             part = jnp.zeros((slice_q, width), F32)
             for k in (0, 1):
                 if z_partners:
@@ -220,7 +222,7 @@
                 part = part + folded(jnp.dot(wide(total), grads, preferred_element_type=F32))
         else:
             part = jnp.zeros((slice_q, width), F32)
-            for some in (groups[:2], groups[2:]):
+            for some in (groups[:2], groups[2:3], groups[3:]):
                 there = [z_at(d) for group in some for d in group]
                 for group in some:
                     for d in group:
@@ -244,9 +246,6 @@
         if sweep == 0:
             applied = omega * applied
         whitened = whitened + omega * (query - applied - DAMP * whitened)
-        if sweep == ITERS - 2:
-            swap[core] = whitened
-            push(swap.at[core], swap.at[core], w_sem.at[0], sibling)
 
     other = x * CORES + 1 - core
     arrived(swap.at[0], w_sem.at[0])

time: 51.2 us -> 51.1 us (level)
  no operation moved by 1% of the time
where the time goes in v12:
time: 51.1 us; the launch traced here: 51 us
  Pallas kernels  50.4 us (99%)
  local copies, waits for them, and re-layouts  0.6 us (1%)
    pallas_call x1, Pallas kernels, body(): pl.pallas_call(functools.partial(kernel, n_grp, n_z, omega, total_rows),...  50.4 us

profile of v12, /device:TPU:1, one launch (start us, length us, event | category | flops | bytes accessed | tf_op | source)
XLA Modules:
  0.0 51.0 jit_solution(8086913418611698586)
XLA Ops:
  0.0 50.4 %influence.1 = f32[16,128]{1,0:T(8,128)S(1)} custom-call(bf16[16,8192]{1,0:T(8,128)(2,1)} %g_ref.1, bf16[256,128]{1,0:T(8,128)(2,1)} %q_ref.1), custom_call_target="tpu_custom_call" | custom-call | tf_op jit(solution)/shard_map/influence/pallas_call | solution.py:309
  50.4 0.6 %copy.4 = f32[16,128]{1,0:T(8,128)} copy(f32[16,128]{1,0:T(8,128)S(1)} %influence.1) | data formatting | bytes 16384

commit v13 on v12

--- a/solution.py
+++ b/solution.py
@@ -136,15 +136,15 @@
                 here = gbuf.at[:, core, z_at(d)]
                 push(here, here, gc_sem.at[d], sibling)
 
-    own_g.wait()
     for group in groups:
         for d in group:
             here = gbuf.at[x, core, z_at(d)]
             if d:
                 arrived(here, gz_sem.at[d])
             for same, _ in x_partners:
-                push(here, here, gx_sem.at[d], same)
+                push(here if d else gl.at[:, cut(z, width)], here, gx_sem.at[d], same)
         if 0 in group:
+            own_g.wait()
             own_q.wait()
             spot = qb.at[(1 - x_lo) * 2 + core]
             arrived(spot, q_sem.at[0])

time: 51.1 us -> 51.1 us (level)
  no operation moved by 1% of the time
where the time goes in v13:
time: 51.1 us; the launch traced here: 51 us
  Pallas kernels  50.4 us (99%)
  local copies, waits for them, and re-layouts  0.6 us (1%)
    pallas_call x1, Pallas kernels, body(): pl.pallas_call(functools.partial(kernel, n_grp, n_z, omega, total_rows),...  50.4 us

profile of v13, /device:TPU:1, one launch (start us, length us, event | category | flops | bytes accessed | tf_op | source)
XLA Modules:
  0.0 51.0 jit_solution(9704123344785348008)
XLA Ops:
  0.0 50.4 %influence.1 = f32[16,128]{1,0:T(8,128)S(1)} custom-call(bf16[16,8192]{1,0:T(8,128)(2,1)} %g_ref.1, bf16[256,128]{1,0:T(8,128)(2,1)} %q_ref.1), custom_call_target="tpu_custom_call" | custom-call | tf_op jit(solution)/shard_map/influence/pallas_call | solution.py:309
  50.4 0.6 %copy.4 = f32[16,128]{1,0:T(8,128)} copy(f32[16,128]{1,0:T(8,128)S(1)} %influence.1) | data formatting | bytes 16384
